TPU v7x, 512 devices: a whole 4x8x8 slice. The times are simulated.
512 devices in a mesh: gx: 32 (over z, x), gy: 16 (over y, core).
Axes of the slice: x: 4, y: 8, z: 8, core: 2. Of those that a mesh axis runs over, the one named last changes fastest.
Arguments:
- iterate: float32 [2, 32, 16, 8, 512], P(None, 'gx', 'gy'), may hold values from -6 to 6
- residual: float32 [2, 32, 16, 8, 512], P(None, 'gx', 'gy'), may hold values from -64 to 64
- direction: float32 [2, 32, 16, 8, 512], P(None, 'gx', 'gy'), may hold values from -64 to 64
- cells: int32 [3, 32, 16, 8, 512], P(None, 'gx', 'gy'), may hold values from 0 to 127, as said below
- fracs: float32 [3, 32, 16, 8, 512], P(None, 'gx', 'gy'), may hold values from 0 to 1
- counts: int32 [32, 16, 8], P('gx', 'gy'), may hold values from 1 to 512, as said below
- slot_tile: int32 [32, 16, 8], P('gx', 'gy'), may hold values from 0 to 7
- spectrum: float32 [256, 256, 256], P('gx', 'gy'), may hold values from 0.2 to 5, as said below
Outputs:
- new_iterate: float32 [2, 32, 16, 8, 512], P(None, 'gx', 'gy')
- new_residual: float32 [2, 32, 16, 8, 512], P(None, 'gx', 'gy')
- new_direction: float32 [2, 32, 16, 8, 512], P(None, 'gx', 'gy')
Inputs may be any that keep to these rules, and one draw needn't show every extreme that they name: `cells`: component 0 of a point's cell lies in 16 * t to 16 * t + 15, t being its block's slot_tile; components 1 and 2 lie in the grid pencil of the device that holds the point. `counts`: slots 0 to count - 1 of a block hold live points, the others are padding; on every device some block has 512 live points. Even: spectrum at index (k0, k1, k2) equals spectrum at ((-k0) mod 256, (-k1) mod 256, (-k2) mod 256).
All inputs are finite; a program needn't handle non-finite values.
Results may differ from a plain program's by a relative error of at most 0.0003.
Values sent between devices are 32-bit elements; how exact they have to be, the bound alone decides.
No kernel may reach another device: no remote copies, remote signals or barrier semaphores. Data moves between devices by JAX's collectives and lax.ppermute only.
A program may use at most 64 MiB of HBM per device.

v0:
```python
import math

import jax
import jax.numpy as jnp
from jax import lax
from jax.sharding import PartitionSpec as P

G = 128
TL = 16


noise_var = 0.5
highest = lax.Precision.HIGHEST


def extended_2(cells, sides, width):
    for axis, dim in sides:
        count = lax.axis_size(axis)
        ends = count - 1
        head = lax.slice_in_dim(cells, 0, width, axis=dim)
        tail = lax.slice_in_dim(cells, cells.shape[dim] - width, cells.shape[dim], axis=dim)
        cells = jnp.concatenate(
            [
                lax.ppermute(tail, axis, [(i, (i + 1) % count) for i in range(ends)]),
                cells,
                lax.ppermute(head, axis, [((i + 1) % count, i) for i in range(ends)]),
            ],
            axis=dim,
        )
    return cells


def cubic_taps(fraction):
    frac_sq = fraction * fraction
    frac_cube = frac_sq * fraction
    return (
        -0.5 * frac_cube + frac_sq - 0.5 * fraction,
        1.5 * frac_cube - 2.5 * frac_sq + 1.0,
        -1.5 * frac_cube + 2.0 * frac_sq + 0.5 * fraction,
        0.5 * frac_cube - 0.5 * frac_sq,
    )


def stencil(first_cell, fraction, extent):
    places = lax.broadcasted_iota(jnp.int32, (first_cell.shape[0], extent, first_cell.shape[1]), 1)
    tap_values = cubic_taps(fraction)
    result = jnp.zeros(places.shape, fraction.dtype)
    for offset in range(4):
        result = result + jnp.where(
            places == (first_cell + offset)[:, None, :], tap_values[offset][:, None, :], 0.0
        )
    return result


def slot_weights(
    cell_index, fraction, tile_index, live_mask, start_one, start_two, wide_one, wide_two
):
    depth = (
        stencil(cell_index[0] - tile_index[:, None] * TL, fraction[0], TL + 3)
        * live_mask[:, None, :]
    )
    across = stencil(cell_index[1] - start_one + 1, fraction[1], wide_one + 4)
    upward = stencil(cell_index[2] - start_two + 1, fraction[2], wide_two + 4)
    plane = across[:, :, None, :] * upward[:, None, :, :]
    return (depth, plane.reshape(plane.shape[0], (wide_one + 4) * (wide_two + 4), plane.shape[3]))


def dft_table(rows_out, cols_in, length, sign, factor):
    row_ids = lax.broadcasted_iota(jnp.int32, (rows_out, cols_in), 0)
    col_ids = lax.broadcasted_iota(jnp.int32, (rows_out, cols_in), 1)
    angle = (row_ids * col_ids % length).astype(jnp.float32) * (2.0 * math.pi / length)
    return (jnp.cos(angle) * factor, sign * jnp.sin(angle) * factor)


def along_axis(table, packed, form):
    real_table, imag_table = table
    real_part = jnp.einsum(form, real_table, packed[0], precision=highest) - jnp.einsum(
        form, imag_table, packed[1], precision=highest
    )
    imag_part = jnp.einsum(form, real_table, packed[1], precision=highest) + jnp.einsum(
        form, imag_table, packed[0], precision=highest
    )
    return jnp.stack([real_part, imag_part])


def fold_rims(extended, axis, wide):
    middle_part = lax.slice_in_dim(extended, 4, wide + 4, axis=axis)
    lower_rim = lax.slice_in_dim(extended, 0, 2, axis=axis)
    upper_rim = lax.slice_in_dim(extended, wide + 6, wide + 8, axis=axis)
    low_pad = [(0, 0)] * extended.ndim
    low_pad[axis] = (0, wide - 2)
    high_pad = [(0, 0)] * extended.ndim
    high_pad[axis] = (wide - 2, 0)
    return middle_part + jnp.pad(lower_rim, low_pad) + jnp.pad(upper_rim, high_pad)


def on_device(iterate, residual, direction, cells, fracs, counts, slot_tile, spectrum):
    probes = direction.shape[0]
    slots_n = direction.shape[3]
    cap_n = direction.shape[4]
    wide_one = G // lax.axis_size("gx")
    wide_two = G // lax.axis_size("gy")
    length = 2 * G
    span = TL + 3
    tiles_n = G // TL
    group_size = 4
    groups_n = slots_n // group_size
    columns = (wide_one + 4) * (wide_two + 4)
    start_one = lax.axis_index("gx") * wide_one
    start_two = lax.axis_index("gy") * wide_two
    live_mask = (
        lax.broadcasted_iota(jnp.int32, (slots_n, cap_n), 1) < counts[0, 0][:, None]
    ).astype(jnp.float32)
    masked_dir = direction[:, 0, 0] * live_mask[None]
    masked_res = residual[:, 0, 0] * live_mask[None]
    cell_groups = cells[:, 0, 0].reshape(3, groups_n, group_size, cap_n).transpose(1, 0, 2, 3)
    frac_groups = fracs[:, 0, 0].reshape(3, groups_n, group_size, cap_n).transpose(1, 0, 2, 3)
    tile_groups = slot_tile[0, 0].reshape(groups_n, group_size)
    live_groups = live_mask.reshape(groups_n, group_size, cap_n)
    pick_groups = (
        tile_groups[:, :, None] == jnp.arange(tiles_n, dtype=jnp.int32)[None, None, :]
    ).astype(jnp.float32)
    dir_groups = masked_dir.reshape(probes, groups_n, group_size, cap_n).transpose(1, 0, 2, 3)

    def fetch_weights(source):
        cell_index, fraction, tile_index, mask_row = source
        return slot_weights(
            cell_index, fraction, tile_index, mask_row, start_one, start_two, wide_one, wide_two
        )

    sources = (cell_groups, frac_groups, tile_groups, live_groups)

    def spread_group(totals, item):
        source, tile_pick, values = item
        depth, plane = fetch_weights(source)
        weighted = depth[None] * values[:, :, None, :]
        contrib = jnp.einsum("rsap,smp->rsam", weighted, plane, precision=highest)
        return (totals + jnp.einsum("st,rsam->rtam", tile_pick, contrib, precision=highest), None)

    start_totals = jnp.zeros((probes, tiles_n, span, columns), jnp.float32)
    totals, unused = lax.scan(spread_group, start_totals, (sources, pick_groups, dir_groups))
    window = jnp.zeros((probes, G + 3, columns), jnp.float32)
    for tile_num in range(tiles_n):
        window = window.at[:, tile_num * TL : tile_num * TL + span].add(totals[:, tile_num])
    window = window.reshape(probes, G + 3, wide_one + 4, wide_two + 4)
    extended = extended_2(window, (("gx", 2), ("gy", 3)), 2)
    folded = fold_rims(fold_rims(extended, 3, wide_two), 2, wide_one)
    field = folded[:, 1 : G + 1]
    forward = dft_table(length, G, length, -1.0, 1.0)
    inverse = dft_table(G, length, length, 1.0, 1.0 / length)
    packed = jnp.stack(
        [
            jnp.einsum("kn,rnij->rkij", forward[0], field, precision=highest),
            jnp.einsum("kn,rnij->rkij", forward[1], field, precision=highest),
        ]
    )
    turned = lax.all_to_all(packed, "gx", split_axis=2, concat_axis=3, tiled=True)
    turned = along_axis(forward, turned, "kn,ranj->rakj")
    turned = lax.all_to_all(turned, "gy", split_axis=3, concat_axis=4, tiled=True)
    turned = along_axis(forward, turned, "kn,rabn->rabk") * spectrum[None, None]
    turned = along_axis(inverse, turned, "kn,rabn->rabk")
    turned = lax.all_to_all(turned, "gy", split_axis=4, concat_axis=3, tiled=True)
    turned = along_axis(inverse, turned, "kn,ranj->rakj")
    turned = lax.all_to_all(turned, "gx", split_axis=3, concat_axis=2, tiled=True)
    smooth = jnp.einsum("kn,rnij->rkij", inverse[0], turned[0], precision=highest) - jnp.einsum(
        "kn,rnij->rkij", inverse[1], turned[1], precision=highest
    )
    padded = jnp.pad(smooth, ((0, 0), (1, 2), (0, 0), (0, 0)))
    halo_grid = extended_2(padded, (("gx", 2), ("gy", 3)), 2).reshape(probes, G + 3, columns)
    blocks = jnp.stack(
        [halo_grid[:, tile_num * TL : tile_num * TL + span] for tile_num in range(tiles_n)], axis=1
    )

    def read_group(item):
        source, tile_pick = item
        depth, plane = fetch_weights(source)
        picked = jnp.einsum("st,rtam->rsam", tile_pick, blocks, precision=highest)
        partial_h = jnp.einsum("rsam,smp->rsap", picked, plane, precision=highest)
        return jnp.sum(partial_h * depth[None], axis=2)

    gathered = lax.map(read_group, (sources, pick_groups))
    interp = gathered.transpose(1, 0, 2, 3).reshape(probes, slots_n, cap_n)
    image = interp + noise_var * masked_dir
    old_norm = lax.psum(jnp.sum(masked_res * masked_res, axis=(1, 2)), ("gx", "gy"))
    curvature = lax.psum(jnp.sum(masked_dir * image, axis=(1, 2)), ("gx", "gy"))
    alpha = old_norm / curvature
    new_residual = masked_res - alpha[:, None, None] * image
    new_norm = lax.psum(jnp.sum(new_residual * new_residual, axis=(1, 2)), ("gx", "gy"))
    new_iterate = iterate[:, 0, 0] * live_mask[None] + alpha[:, None, None] * masked_dir
    beta = new_norm / old_norm
    new_direction = new_residual + beta[:, None, None] * masked_dir
    return (new_iterate[:, None, None], new_residual[:, None, None], new_direction[:, None, None])


def solution(mesh):
    placed = (
        P(None, "gx", "gy", None, None),
        P(None, "gx", "gy", None, None),
        P(None, "gx", "gy", None, None),
        P(None, "gx", "gy", None, None),
        P(None, "gx", "gy", None, None),
        P("gx", "gy", None),
        P("gx", "gy", None),
        P("gx", "gy", None),
    )
    return jax.shard_map(
        on_device,
        mesh=mesh,
        in_specs=placed,
        out_specs=(
            P(None, "gx", "gy", None, None),
            P(None, "gx", "gy", None, None),
            P(None, "gx", "gy", None, None),
        ),
        check_vma=False,
    )
```

profile of v0, /device:TPU:1, one launch (start us, length us, event | category | flops | bytes accessed | tf_op | source)
XLA Modules:
  0.0 387.6 jit_solution(12517333516676091555)
XLA Ops:
  6.6 4.3 %while.36 = (s32[]{:T(128)}, f32[2,8,19,96]{3,1,2,0:T(8,128)S(1)}, s32[2,3,4,512]{3,2,1,0:T(4,128)S(1)}, s32[]{:T(128)}, f32[2,3,4,512]{3,2,1,0:T(4,128)S(1)}, /...) while((s32[]{:T(128)}, f32[2,8,19,96]{3,1,2,0:T(8,128)S(1)}, ...), condition=%wide.region_3.4_spmd.clone, body=%wide.region_2.3_spmd.clone.sunk | while | flops 92437512 | bytes 3167499 | solution.py:141
  11.4 4.0 %collective-permute-start = (f32[2,131,2,12]{1,3,2,0:T(8,128)S(1)}, f32[2,131,2,12]{1,3,2,0:T(8,128)S(1)}, u32[]{:S(2)}, u32[]{:S(2)}) collective-permute-start(f32[2,131,2,12]{1,3,2,0:T(8,128)S(1)} %copy.174), channel_id=1, source_target_pairs={{0,16},{16,32},{32,48},{48,64},{64,80},{80,96},{96,112},{112,128},... | collective-permute-start | bytes 75464 | tf_op jit(solution)/shard_map/ppermute | solution.py:24
  16.8 3.7 collective-permute-done.1
  20.5 5.2 %collective-permute-start.2 = (f32[2,131,12,2]{1,3,2,0:T(2,128)S(1)}, f32[2,131,12,2]{1,3,2,0:T(2,128)S(1)}, u32[]{:S(2)}, u32[]{:S(2)}) collective-permute-start(f32[2,131,12,2]{1,3,2,0:T(2,128)S(1)} %get-tuple-element.600), channel_id=1, source_target_pairs={{0,1},{1,2},{2,3},{3,4},{4,5},{5,6},{6,7},{7,8},{8,9},{9,10},{10,1... | collective-permute-start | bytes 75464 | tf_op jit(solution)/shard_map/ppermute | solution.py:24
  25.7 3.4 collective-permute-start.3
  29.1 2.0 collective-permute-done.3
  34.0 2.4 reshape.1270
  36.4 24.5 %all_to_all.60 = f32[32,1,1024]{2,1,0:T(1,128)S(1)} all-to-all(f32[32,1,1024]{2,1,0:T(1,128)S(1)} %reshape.1270), channel_id=1, replica_groups=mesh['gx'=32,'gy'=16] {'gx'}, dimensions={0} | all-to-all | bytes 262144 | tf_op jit(solution)/shard_map/all_to_all | solution.py:157
  62.4 3.9 reshape.1271
  66.3 3.0 copy.147
  70.5 1.7 copy.101
  76.6 4.3 %copy.107 = f32[2,2,8,256,8]{4,2,1,0,3:T(8,128)} copy(f32[2,2,8,256,8]{3,4,2,1,0:T(8,128)S(1)} %pad_maximum_fusion) | data formatting | bytes 524288 | tf_op jit(solution)/shard_map/stack | solution.py:83
  80.9 3.8 reshape.1272
  84.7 20.1 %all_to_all.61 = f32[16,1,4096]{2,1,0:T(1,128)S(1)} all-to-all(f32[16,1,4096]{2,1,0:T(1,128)S(1)} %reshape.1272), channel_id=1, replica_groups=mesh['gx'=32,'gy'=16] {'gy'}, dimensions={0} | all-to-all | bytes 524288 | tf_op jit(solution)/shard_map/all_to_all | solution.py:159
  106.0 3.6 reshape.1273
  109.6 3.7 copy.108
  113.4 2.0 fusion.65
  115.4 2.0 fusion.66
  117.4 2.0 fusion.57
  119.4 2.0 fusion.56
  125.0 1.8 copy.113
  127.6 14.6 %all_to_all.62 = f32[16,1,4096]{2,1,0:T(1,128)S(1)} all-to-all(f32[16,1,4096]{2,1,0:T(1,128)S(1)} %reshape.1274), channel_id=1, replica_groups=mesh['gx'=32,'gy'=16] {'gy'}, dimensions={0} | all-to-all | bytes 524288 | tf_op jit(solution)/shard_map/all_to_all | solution.py:162
  150.0 1.8 copy.117
  152.9 13.3 %all_to_all.63 = f32[32,1,1024]{2,1,0:T(1,128)S(1)} all-to-all(f32[32,1,1024]{2,1,0:T(1,128)S(1)} %reshape.1276), channel_id=1, replica_groups=mesh['gx'=32,'gy'=16] {'gx'}, dimensions={0} | all-to-all | bytes 262144 | tf_op jit(solution)/shard_map/all_to_all | solution.py:164
  172.7 1.9 collective-permute-start.4
  176.0 3.3 collective-permute-done.5
  179.3 3.8 collective-permute-start.6
  183.1 1.9 collective-permute-start.7
  185.1 3.2 collective-permute-done.7
  190.4 3.4 while.35
  194.0 97.8 %all-reduce.5 = (f32[2]{0:T(128)S(1)}, f32[2]{0:T(128)S(1)}) all-reduce(f32[2]{0:T(128)S(1)} %get-tuple-element.501, f32[2]{0:T(128)S(1)} %get-tuple-element.500), channel_id=1, replica_groups=mesh['gx'=32,'gy'=16] {'gx','gy'}, use_global_device_ids=true, to_apply=%region_1.2 | all-reduce | flops 4 | bytes 32 | tf_op jit(solution)/shard_map/psum | solution.py:184
  292.0 94.4 %psum.23 = f32[2]{0:T(128)S(1)} all-reduce(f32[2]{0:T(128)S(1)} %multiply_reduce_fusion), channel_id=1, replica_groups=mesh['gx'=32,'gy'=16] {'gx','gy'}, use_global_device_ids=true, to_apply=%region_10.11 | all-reduce | flops 2 | bytes 16 | tf_op jit(solution)/shard_map/psum | solution.py:188
  (175 shorter events, 50.4 us)
Async XLA Ops:
  10.9 20.3 %copy-start.5 = (pred[4]{0:T(512)(128)(4,1)S(1)}, pred[4]{0:T(512)(128)(4,1)}, u32[]{:S(2)}) copy-start(pred[4]{0:T(512)(128)(4,1)} %constant.475.clone.1) | copy-start | bytes 16
  11.4 5.3 %collective-permute-start = (f32[2,131,2,12]{1,3,2,0:T(8,128)S(1)}, f32[2,131,2,12]{1,3,2,0:T(8,128)S(1)}, u32[]{:S(2)}, u32[]{:S(2)}) collective-permute-start(f32[2,131,2,12]{1,3,2,0:T(8,128)S(1)} %copy.174), channel_id=1, source_target_pairs={{0,16},{16,32},{32,48},{48,64},{64,80},{80,96},{96,112},{112,128},... | collective-permute-start | bytes 75464 | tf_op jit(solution)/shard_map/ppermute | solution.py:24
  15.4 5.0 %collective-permute-start.1 = (f32[2,131,2,12]{1,3,2,0:T(8,128)S(1)}, f32[2,131,2,12]{1,3,2,0:T(8,128)S(1)}, u32[]{:S(2)}, u32[]{:S(2)}) collective-permute-start(f32[2,131,2,12]{1,3,2,0:T(8,128)S(1)} %copy.175), channel_id=1, source_target_pairs={{16,0},{32,16},{48,32},{64,48},{80,64},{96,80},{112,96},{128,112},... | collective-permute-start | bytes 75464 | tf_op jit(solution)/shard_map/ppermute | solution.py:26
  20.5 8.6 %collective-permute-start.2 = (f32[2,131,12,2]{1,3,2,0:T(2,128)S(1)}, f32[2,131,12,2]{1,3,2,0:T(2,128)S(1)}, u32[]{:S(2)}, u32[]{:S(2)}) collective-permute-start(f32[2,131,12,2]{1,3,2,0:T(2,128)S(1)} %get-tuple-element.600), channel_id=1, source_target_pairs={{0,1},{1,2},{2,3},{3,4},{4,5},{5,6},{6,7},{7,8},{8,9},{9,10},{10,1... | collective-permute-start | bytes 75464 | tf_op jit(solution)/shard_map/ppermute | solution.py:24
  25.7 5.4 %collective-permute-start.3 = (f32[2,131,12,2]{1,3,2,0:T(2,128)S(1)}, f32[2,131,12,2]{1,3,2,0:T(2,128)S(1)}, u32[]{:S(2)}, u32[]{:S(2)}) collective-permute-start(f32[2,131,12,2]{1,3,2,0:T(2,128)S(1)} %get-tuple-element.601), channel_id=1, source_target_pairs={{1,0},{2,1},{3,2},{4,3},{5,4},{6,5},{7,6},{8,7},{9,8},{10,9},{11,1... | collective-permute-start | bytes 75464 | tf_op jit(solution)/shard_map/ppermute | solution.py:26
  115.4 6.0 %copy-start.2 = (f32[8,16,256]{2,1,0:T(8,128)S(1)}, f32[8,16,256]{2,1,0:T(8,128)}, u32[]{:S(2)}) copy-start(f32[8,16,256]{2,1,0:T(8,128)} %param.35) | copy-start | bytes 393220
  170.6 14.4 %copy-start.4 = (s32[1,1,8]{2,1,0:T(1,128)S(1)}, s32[1,1,8]{2,1,0:T(1,128)}, u32[]{:S(2)}) copy-start(s32[1,1,8]{2,1,0:T(1,128)} %param.33) | copy-start | bytes 100
  172.7 3.2 collective-permute-start.4
  174.6 4.7 %collective-permute-start.5 = (f32[2,131,2,8]{1,3,2,0:T(8,128)S(1)}, f32[2,131,2,8]{1,3,2,0:T(8,128)S(1)}, u32[]{:S(2)}, u32[]{:S(2)}) collective-permute-start(f32[2,131,2,8]{1,3,2,0:T(8,128)S(1)} %get-tuple-element.618), channel_id=1, source_target_pairs={{16,0},{32,16},{48,32},{64,48},{80,64},{96,80},{112,96},{128,112},... | collective-permute-start | bytes 50312 | tf_op jit(solution)/shard_map/ppermute | solution.py:26
  179.3 5.8 %collective-permute-start.6 = (f32[2,131,8,2]{1,3,2,0:T(2,128)S(1)}, f32[2,131,8,2]{1,3,2,0:T(2,128)S(1)}, u32[]{:S(2)}, u32[]{:S(2)}) collective-permute-start(f32[2,131,8,2]{1,3,2,0:T(2,128)S(1)} %get-tuple-element.614), channel_id=1, source_target_pairs={{0,1},{1,2},{2,3},{3,4},{4,5},{5,6},{6,7},{7,8},{8,9},{9,10},{10,1... | collective-permute-start | bytes 50312 | tf_op jit(solution)/shard_map/ppermute | solution.py:24
  183.1 5.2 %collective-permute-start.7 = (f32[2,131,8,2]{1,3,2,0:T(2,128)S(1)}, f32[2,131,8,2]{1,3,2,0:T(2,128)S(1)}, u32[]{:S(2)}, u32[]{:S(2)}) collective-permute-start(f32[2,131,8,2]{1,3,2,0:T(2,128)S(1)} %get-tuple-element.615), channel_id=1, source_target_pairs={{1,0},{2,1},{3,2},{4,3},{5,4},{6,5},{7,6},{8,7},{9,8},{10,9},{11,1... | collective-permute-start | bytes 50312 | tf_op jit(solution)/shard_map/ppermute | solution.py:26
  190.3 3.4 copy-start
  190.4 3.4 copy-start.1
  190.4 196.1 %copy-start.3 = (f32[2,1,1,8,512]{4,3,2,1,0:T(8,128)S(1)}, f32[2,1,1,8,512]{4,3,2,1,0:T(8,128)}, u32[]{:S(2)}) copy-start(f32[2,1,1,8,512]{4,3,2,1,0:T(8,128)} %param.28) | copy-start | bytes 98308
where the time goes:
time: 394 us; the launch traced here: 388 us
  blocking collectives  265 us (67%)
  local copies, waits for them, and re-layouts  49.2 us (12%)
  matrix products  25.8 us (7%)
  starting transfers between devices  22.7 us (6%)
  waiting for transfers between devices  12.2 us (3%)
  other arithmetic  10.9 us (3%)
    psum x1, blocking collectives, on_device(): lax.psum(jnp.sum(masked_res * masked_res, axis=(1, 2)), ('gx', 'gy'))  97.8 us
    psum x1, blocking collectives, on_device(): lax.psum(jnp.sum(new_residual * new_residual, axis=(1, 2)), ('gx', 'gy'))  94.4 us
    all_to_all x1, blocking collectives, on_device(): lax.all_to_all(packed, 'gx', split_axis=2, concat_axis=3, tiled=True)  24.5 us
    all_to_all x1, blocking collectives, on_device(): lax.all_to_all(turned, 'gy', split_axis=3, concat_axis=4, tiled=True)  20.1 us
    unnamed x26, local copies, waits for them, and re-layouts  18.7 us
    ppermute x4, starting transfers between devices, extended_2(): lax.ppermute(tail, axis, [(i, (i + 1) % count) for i in range(ends)])  14.8 us
    all_to_all x1, blocking collectives, on_device(): lax.all_to_all(turned, 'gy', split_axis=4, concat_axis=3, tiled=True)  14.6 us
    all_to_all x1, blocking collectives, on_device(): lax.all_to_all(turned, 'gx', split_axis=3, concat_axis=2, tiled=True)  13.3 us
  transfers between devices with their start and end apart: 8, of which 4 were waited for; matrix products, arithmetic and copies ran while one was open for 0% of the time, Pallas kernels for 0%

commit v1 on v0

v1 whole, which is shorter than its diff:
```python
import functools
import math

import jax
import jax.numpy as jnp
import ml_dtypes
import numpy as np
from jax import lax
from jax.experimental import pallas as pl
from jax.experimental.pallas import tpu as pltpu
from jax.sharding import PartitionSpec as P

G = 128
LENGTH = 2 * G
TL = 16
SPAN = 24
NX = 32
NY = 16
WIDE_ONE = G // NX
WIDE_TWO = G // NY
WIN_ONE = WIDE_ONE + 3
WIN_TWO = WIDE_TWO + 3
PAD_ONE = 8
PAD_TWO = 16
K_ONE = LENGTH // NX
K_TWO = LENGTH // NY
PARTS_X = 2 * WIN_ONE
ROWS_X = 10
EXTRA_X = PARTS_X - ROWS_X
HALF = PAD_TWO - WIN_TWO
ROWS_Y = 2 * WIN_TWO
LANES = 128
WIN_ROWS = 144
NOISE = 0.5
VMEM_LIMIT = 24 * 1024 * 1024
f32 = jnp.float32
bf16 = jnp.bfloat16


def rotation(out_index, in_index, sign, scale):
    turns = (np.outer(out_index, in_index) % LENGTH).astype(np.float64)
    angle = turns * (2.0 * math.pi / LENGTH)
    return np.cos(angle) * scale, sign * np.sin(angle) * scale


def complex_table(out_index, out_part, out_ok, in_index, in_part, in_ok, sign, scale):
    real, imag = rotation(out_index, in_index, sign, scale)
    same = out_part[:, None] == in_part[None, :]
    crossed = np.where(out_part[:, None] == 1, imag, -imag)
    table = np.where(same, real, crossed)
    table = np.where(out_ok[:, None] & in_ok[None, :], table, 0.0)
    high = table.astype(ml_dtypes.bfloat16)
    low = (table - high.astype(np.float64)).astype(ml_dtypes.bfloat16)
    return np.concatenate([high, low], axis=0)


def window_index(owner, offset, wide):
    cell = owner * wide + offset - 1
    return cell, (cell >= 0) & (cell < G)


@functools.lru_cache(None)
def tables():
    def grid(*sizes):
        return [part.reshape(-1) for part in np.meshgrid(*[np.arange(size) for size in sizes], indexing="ij")]

    yes = lambda rows: np.ones(rows.shape, bool)
    n1_part, n1 = grid(2, G)
    k1_part, k1_low, k1_owner = grid(2, K_ONE, NX)
    k1 = k1_owner * K_ONE + k1_low
    x_part, x_cell, x_owner = grid(2, WIN_ONE, NX)
    n2, n2_ok = window_index(x_owner, x_cell, WIDE_ONE)
    came = np.concatenate(
        [
            (np.arange(NX)[:, None] + NX * np.arange(ROWS_X)[None, :]).reshape(-1),
            np.arange(NX * ROWS_X, NX * PARTS_X),
        ]
    )
    k2_part, k2_low, k2_owner = grid(2, K_TWO, NY)
    k2 = k2_owner * K_TWO + k2_low
    y_owner, y_cell, y_part = grid(NY, WIN_TWO, 2)
    n3, n3_ok = window_index(y_owner, y_cell, WIDE_TWO)
    k3_part, k3 = grid(2, LENGTH)
    return (
        complex_table(k1, k1_part, yes(k1), n1, n1_part, yes(n1), -1.0, 1.0),
        complex_table(k2, k2_part, yes(k2), n2[came], x_part[came], n2_ok[came], -1.0, 1.0),
        complex_table(k3, k3_part, yes(k3), n3, y_part, n3_ok, -1.0, 1.0),
        complex_table(n3, y_part, n3_ok, k3, k3_part, yes(k3), 1.0, 1.0 / LENGTH),
        complex_table(n2, x_part, n2_ok, k2, k2_part, yes(k2), 1.0, 1.0 / LENGTH),
        complex_table(n1, n1_part, yes(n1), k1, k1_part, yes(k1), 1.0, 1.0 / LENGTH),
    )


def split(value):
    high = value.astype(bf16)
    return high, (value - high.astype(f32)).astype(bf16)


def dot(left, right, dims=((1,), (0,))):
    return lax.dot_general(left, right, (dims, ((), ())), preferred_element_type=f32)


def transform(table_ref, data):
    rows = table_ref.shape[0] // 2
    data_high, data_low = split(data)
    both = dot(table_ref[:rows], jnp.concatenate([data_high, data_low], axis=1))
    return both[:, :LANES] + both[:, LANES:] + dot(table_ref[rows:], data_high)


def exchange(arrays, block):
    lane = lax.broadcasted_iota(jnp.int32, arrays[0].shape, 1)
    step = 1
    while step < len(arrays):
        width = step * block
        low = (lane // width) % 2 == 0
        mixed = list(arrays)
        for place in range(len(arrays)):
            if place & step:
                continue
            first, second = arrays[place], arrays[place | step]
            mixed[place] = jnp.where(low, first, pltpu.roll(second, width, 1))
            mixed[place | step] = jnp.where(low, pltpu.roll(first, LANES - width, 1), second)
        arrays = mixed
        step *= 2
    return arrays


def lane_cell(shape):
    return lax.broadcasted_iota(jnp.int32, shape, 1) % PAD_TWO


def pack(rows):
    cell = lane_cell(rows[0].shape)
    message = list(rows[:ROWS_X])
    for extra, row in enumerate(rows[ROWS_X:]):
        for half in range(2):
            moved = pltpu.roll(row, WIN_TWO - half * HALF, 1)
            place = 2 * extra + half
            message[place] = jnp.where(cell >= WIN_TWO, moved, message[place])
        place = 2 * EXTRA_X
        message[place] = jnp.where(cell == WIN_TWO + extra, pltpu.roll(row, 1 + extra, 1), message[place])
    return message


def unpack(message):
    cell = lane_cell(message[0].shape)
    rows = []
    for extra in range(EXTRA_X):
        row = pltpu.roll(message[2 * EXTRA_X], LANES - 1 - extra, 1)
        for half in (1, 0):
            moved = pltpu.roll(message[2 * extra + half], LANES - WIN_TWO + half * HALF, 1)
            row = jnp.where(cell < (half + 1) * HALF, moved, row)
        rows.append(row)
    return rows


def gather(ref, row, count, stride):
    return ref[pl.ds(row, count, stride=stride), :]


def live_slots(count_ref, shape):
    slot = lax.broadcasted_iota(jnp.int32, shape, 0)
    limit = jnp.zeros(shape, jnp.int32)
    for index in range(shape[0]):
        limit = jnp.where(slot == index, count_ref[0, 0, index], limit)
    return lax.broadcasted_iota(jnp.int32, shape, 1) < limit


def cubic_taps(fraction):
    frac_sq = fraction * fraction
    frac_cube = frac_sq * fraction
    return (
        -0.5 * frac_cube + frac_sq - 0.5 * fraction,
        1.5 * frac_cube - 2.5 * frac_sq + 1.0,
        -1.5 * frac_cube + 2.0 * frac_sq + 0.5 * fraction,
        0.5 * frac_cube - 0.5 * frac_sq,
    )


def stencil(first, taps, slot, extent):
    first_row = first[slot : slot + 1]
    offset = lax.broadcasted_iota(jnp.int32, (extent, first.shape[1]), 0) - first_row
    result = jnp.zeros(offset.shape, f32)
    for index in range(4):
        result = jnp.where(offset == index, taps[index][slot : slot + 1], result)
    return result


def point_weights(cells_ref, fracs_ref):
    firsts = [cells_ref[dim, 0, 0] & (wide - 1) for dim, wide in enumerate((TL, WIDE_ONE, WIDE_TWO))]
    taps = [cubic_taps(fracs_ref[dim, 0, 0]) for dim in range(3)]

    def weights(slot):
        depth = stencil(firsts[0], taps[0], slot, SPAN)
        across = stencil(firsts[1], taps[1], slot, PAD_ONE)
        upward = stencil(firsts[2], taps[2], slot, PAD_TWO)
        plane = across[:, None, :] * upward[None, :, :]
        return depth, plane.reshape(LANES, plane.shape[2])

    return weights


def spread_kernel(*refs):
    outside, refs = refs[:6], refs[6:]
    out_ref, masked_ref, live_ref, depth_ref, plane_high_ref, plane_low_ref, *inside, win_ref, sems = refs
    tile_ref, count_ref, dir_ref, cells_ref, fracs_ref, table_ref = inside
    copies = [pltpu.make_async_copy(far, near, sems.at[at]) for at, (far, near) in enumerate(zip(outside, inside))]
    for copy in copies:
        copy.start()
    win_ref[...] = jnp.zeros_like(win_ref)
    for copy in copies[:5]:
        copy.wait()
    probes, slots = dir_ref.shape[0], dir_ref.shape[3]
    live = live_slots(count_ref, dir_ref.shape[3:])
    live_ref[...] = live.astype(f32)
    masked = [jnp.where(live, dir_ref[probe, 0, 0], 0.0) for probe in range(probes)]
    for probe in range(probes):
        masked_ref[probe] = masked[probe]
    weights = point_weights(cells_ref, fracs_ref)
    for slot in range(slots):
        depth, plane = weights(slot)
        plane_high, plane_low = split(plane)
        depth_ref[slot], plane_high_ref[slot], plane_low_ref[slot] = depth, plane_high, plane_low
        values = jnp.concatenate([depth * masked[probe][slot : slot + 1] for probe in range(probes)], axis=0)
        value_high, value_low = split(values)
        rows = values.shape[0]
        first = dot(jnp.concatenate([value_high, value_low], axis=0), plane_high, ((1,), (1,)))
        total = first[:rows] + first[rows:] + dot(value_high, plane_low, ((1,), (1,)))
        place = pl.ds(pl.multiple_of(tile_ref[0, 0, slot] * TL, TL), SPAN)
        for probe in range(probes):
            win_ref[probe, place, :] += total[probe * SPAN : (probe + 1) * SPAN]
    field = jnp.concatenate([win_ref[0, 1 : G + 1, :], win_ref[1, 1 : G + 1, :]], axis=0)
    for copy in copies[5:]:
        copy.wait()
    columns = transform(table_ref, field)
    rows = []
    for part in range(2):
        start = part * LENGTH
        pieces = [columns[start + low * NX : start + (low + 1) * NX] for low in range(K_ONE)]
        rows += exchange(pieces, PAD_TWO)[:WIN_ONE]
    for row, piece in enumerate(pack(rows)):
        out_ref[pl.ds(row, NX, stride=ROWS_X), :] = piece


def second_kernel(in_ref, table_ref, out_ref):
    extra = unpack([gather(in_ref, row, NX, ROWS_X) for row in range(2 * EXTRA_X + 1)])
    columns = transform(table_ref, jnp.concatenate([in_ref[...], *extra], axis=0))
    for part in range(2):
        start = part * LENGTH
        pieces = [columns[start + low * NY : start + (low + 1) * NY] for low in range(K_TWO)]
        for cell, piece in enumerate(exchange(pieces, 1)[:WIN_TWO]):
            out_ref[pl.ds(2 * cell + part, NY, stride=ROWS_Y), :] = piece


def third_kernel(in_ref, spec_ref, table_ref, back_ref, out_ref):
    columns = transform(table_ref, in_ref[...])
    factor = spec_ref[...].reshape(LANES, LENGTH).T
    scaled = jnp.concatenate([columns[:LENGTH] * factor, columns[LENGTH:] * factor], axis=0)
    out_ref[...] = transform(back_ref, scaled)


def fourth_kernel(in_ref, table_ref, out_ref):
    parts = []
    for part in range(2):
        pieces = [gather(in_ref, 2 * cell + part, NY, ROWS_Y) for cell in range(WIN_TWO)]
        pieces += [jnp.zeros((NY, LANES), f32)] * (K_TWO - WIN_TWO)
        parts += exchange(pieces, 1)
    columns = transform(table_ref, jnp.concatenate(parts, axis=0))
    rows = [columns[row * NX : (row + 1) * NX] for row in range(PARTS_X)]
    for row, piece in enumerate(pack(rows)):
        out_ref[pl.ds(row, NX, stride=ROWS_X), :] = piece


def read_kernel(
    tile_far_ref, in_ref, res_ref, dir_ref, live_ref, depth_ref, plane_high_ref, plane_low_ref, table_ref,
    image_ref, sums_ref, tile_ref, win_ref, sems,
):
    copy = pltpu.make_async_copy(tile_far_ref, tile_ref, sems.at[0])
    copy.start()
    probes, slots = image_ref.shape[:2]
    rows = [gather(in_ref, row, NX, ROWS_X) for row in range(ROWS_X)]
    rows += unpack(rows)
    parts = []
    for part in range(2):
        pieces = rows[part * WIN_ONE : (part + 1) * WIN_ONE]
        pieces += [jnp.zeros((NX, LANES), f32)] * (PAD_ONE - WIN_ONE)
        parts += exchange(pieces, PAD_TWO)
    smooth = transform(table_ref, jnp.concatenate(parts, axis=0))
    win_ref[...] = jnp.zeros_like(win_ref)
    for probe in range(probes):
        win_ref[probe, 1 : G + 1, :] = smooth[probe * G : (probe + 1) * G]
    copy.wait()
    for slot in range(slots):
        place = pl.ds(pl.multiple_of(tile_ref[0, 0, slot] * TL, TL), SPAN)
        block = jnp.concatenate([win_ref[probe, place, :] for probe in range(probes)], axis=0)
        block_high, block_low = split(block)
        high = plane_high_ref[slot]
        rows = block.shape[0]
        first = dot(jnp.concatenate([block_high, block_low], axis=0), high)
        total = first[:rows] + first[rows:] + dot(block_high, plane_low_ref[slot])
        for probe in range(probes):
            image_ref[probe, slot : slot + 1, :] = jnp.sum(
                depth_ref[slot] * total[probe * SPAN : (probe + 1) * SPAN], axis=0, keepdims=True
            )
    sums = []
    live = live_ref[...]
    for probe in range(probes):
        masked_res, masked_dir = live * res_ref[probe, 0, 0], dir_ref[probe]
        image = live * image_ref[probe] + NOISE * masked_dir
        image_ref[probe] = image
        for left, right in (
            (masked_res, masked_res),
            (masked_dir, image),
            (masked_res, image),
            (image, image),
        ):
            line = jnp.sum(left * right, axis=0, keepdims=True)
            sums.append(sum(line[:, at : at + LANES] for at in range(0, line.shape[1], LANES)))
    column = jnp.sum(jnp.concatenate(sums, axis=0), axis=1, keepdims=True)
    shape = (column.shape[0], LANES)
    own = lax.broadcasted_iota(jnp.int32, shape, 0) == lax.broadcasted_iota(jnp.int32, shape, 1)
    row = jnp.sum(jnp.where(own, column, 0.0), axis=0, keepdims=True)
    sums_ref[...] = jnp.broadcast_to(row, sums_ref.shape)


def total_kernel(in_ref, out_ref):
    out_ref[...] = jnp.broadcast_to(jnp.sum(in_ref[...], axis=0, keepdims=True), out_ref.shape)


def update_kernel(sums_ref, image_ref, live_ref, iterate_ref, res_ref, dir_ref, new_iterate_ref, new_res_ref, new_dir_ref):
    sums = jnp.sum(sums_ref[...], axis=0, keepdims=True)
    live = live_ref[...]
    for probe in range(image_ref.shape[0]):
        old_norm, curvature, crossed, squared = (sums[:, 4 * probe + at : 4 * probe + at + 1] for at in range(4))
        alpha = old_norm / curvature
        new_norm = old_norm + alpha * (alpha * squared - 2.0 * crossed)
        beta = new_norm / old_norm
        masked_dir = dir_ref[probe]
        new_res = live * res_ref[probe, 0, 0] - alpha * image_ref[probe]
        new_iterate_ref[probe, 0, 0] = live * iterate_ref[probe, 0, 0] + alpha * masked_dir
        new_res_ref[probe, 0, 0] = new_res
        new_dir_ref[probe, 0, 0] = new_res + beta * masked_dir


def call(kernel, name, outs, operands, far=0, scratch=()):
    operands = [pltpu.with_memory_space_constraint(operand, pltpu.HBM) for operand in operands[:far]] + [*operands[far:]]
    near = len(operands) - far
    outs = [jax.ShapeDtypeStruct(*(out if isinstance(out[0], tuple) else (out, f32))) for out in outs]
    return pl.pallas_call(
        kernel,
        out_shape=outs,
        in_specs=[pl.BlockSpec(memory_space=pltpu.HBM)] * far + [pl.BlockSpec(memory_space=pltpu.VMEM)] * near,
        out_specs=[pl.BlockSpec(memory_space=pltpu.VMEM)] * len(outs),
        scratch_shapes=list(scratch),
        compiler_params=pltpu.CompilerParams(vmem_limit_bytes=VMEM_LIMIT),
        name=name,
    )(*operands)


def across(axis, value):
    rows = value.shape[0]
    sent = value.reshape(rows, 1, LANES)
    return lax.all_to_all(sent, axis, split_axis=0, concat_axis=0, tiled=True).reshape(rows, LANES)


def on_device(iterate, residual, direction, cells, fracs, counts, slot_tile, spectrum):
    first, second, third, third_back, second_back, first_back = tables()
    probes, slots, cap = direction.shape[0], direction.shape[3], direction.shape[4]
    window = pltpu.VMEM((probes, WIN_ROWS, LANES), f32)
    operands = (slot_tile, counts, direction, cells, fracs, first)
    near = [
        (pltpu.SMEM if at < 2 else pltpu.VMEM)(operand.shape, operand.dtype) for at, operand in enumerate(operands)
    ]
    sent, masked, live, depth, plane_high, plane_low = call(
        spread_kernel,
        "spread",
        [
            (NX * ROWS_X, LANES),
            (probes, slots, cap),
            (slots, cap),
            (slots, SPAN, cap),
            ((slots, LANES, cap), bf16),
            ((slots, LANES, cap), bf16),
        ],
        operands,
        far=len(operands),
        scratch=(*near, window, pltpu.SemaphoreType.DMA((len(operands),))),
    )
    came = across("gx", sent)
    (sent,) = call(second_kernel, "second", [(NY * ROWS_Y, LANES)], (came, second))
    came = across("gy", sent)
    (sent,) = call(third_kernel, "third", [(NY * ROWS_Y, LANES)], (came, spectrum, third, third_back))
    came = across("gy", sent)
    (sent,) = call(fourth_kernel, "fourth", [(NX * ROWS_X, LANES)], (came, second_back))
    came = across("gx", sent)
    image, sums = call(
        read_kernel,
        "read",
        [(probes, slots, cap), (NX, LANES)],
        (slot_tile, came, residual, masked, live, depth, plane_high, plane_low, first_back),
        far=1,
        scratch=(near[0], window, pltpu.SemaphoreType.DMA((1,))),
    )
    sums = across("gx", sums)
    (sums,) = call(total_kernel, "total", [(NY, LANES)], (sums,))
    sums = across("gy", sums)
    return tuple(call(update_kernel, "update", [direction.shape] * 3, (sums, image, live, iterate, residual, masked)))


def solution(mesh):
    points = P(None, "gx", "gy", None, None)
    blocks = P("gx", "gy", None)
    return jax.shard_map(
        on_device,
        mesh=mesh,
        in_specs=(points, points, points, points, points, blocks, blocks, blocks),
        out_specs=(points, points, points),
        check_vma=False,
    )
```

time: 394 us -> 103 us (0.26); the launches traced: 388 us -> 102 us
  blocking collectives: 265 us -> 92.9 us
  local copies, waits for them, and re-layouts: 49.2 us -> 1.26 us
  matrix products: 25.8 us -> 0 us
  starting transfers between devices: 22.7 us -> 0 us
  waiting for transfers between devices: 12.2 us -> 0 us
  other arithmetic: 10.9 us -> 0 us
  Pallas kernels: 0 us -> 7.43 us
    psum x2 -> x0, blocking collectives: 192 us -> none  [the longest x1 97.8 us: on_device(): lax.psum(jnp.sum(masked_res * masked_res, axis=(1, 2)), ('gx', 'gy'))]
    dot_general x28 -> x0, matrix products: 25.8 us -> none  [the longest x4 4.41 us: along_axis(): jnp.einsum(form, imag_table, packed[1], precision=highest)]
    ppermute x8 -> x0, starting transfers between devices: 22.7 us -> none  [the longest x4 14.8 us: extended_2(): lax.ppermute(tail, axis, [(i, (i + 1) % count) for i in range(ends)])]
    all_to_all x4 -> x6, blocking collectives: 72.5 us -> 92.9 us  [across(): lax.all_to_all(sent, axis, split_axis=0, concat_axis=0, tiled=True)]
    unnamed x26 -> x16, local copies, waits for them, and re-layouts: 18.7 us -> 1.26 us
    another operation x18 -> x0, local copies, waits for them, and re-layouts: 12.7 us -> none  [the longest x3 7.97 us: along_axis(): return jnp.stack([real_part, imag_part])]
    ppermute x8 -> x0, waiting for transfers between devices: 12.2 us -> none  [the longest x4 12.2 us: extended_2(): lax.ppermute(head, axis, [((i + 1) % count, i) for i in range(ends)])]
    all_to_all x5 -> x0, local copies, waits for them, and re-layouts: 8.6 us -> none  [the longest x1 3.73 us: on_device(): lax.all_to_all(turned, 'gy', split_axis=3, concat_axis=4, tiled=True)]
  transfers between devices with their start and end apart: 8 -> 0, of which waited for: 4 -> 0; matrix products, arithmetic and copies ran while one was open for 0% -> 0% of each run, Pallas kernels for 0% -> 0%
where the time goes in v1:
time: 103 us; the launch traced here: 102 us
  blocking collectives  92.9 us (90%)
  Pallas kernels  7.43 us (7%)
  local copies, waits for them, and re-layouts  1.26 us (1%)
    all_to_all x6, blocking collectives, across(): lax.all_to_all(sent, axis, split_axis=0, concat_axis=0, tiled=True)  92.9 us
    pallas_call x7, Pallas kernels, call(): pl.pallas_call(kernel, out_shape=outs, in_specs=[pl.BlockSpec(memory_spac...  7.43 us

profile of v1, /device:TPU:1, one launch (start us, length us, event | category | flops | bytes accessed | tf_op | source)
XLA Modules:
  0.0 102.3 jit_solution(18417943123375290299)
XLA Ops:
  0.6 2.6 %spread.1 = (f32[320,128]{1,0:T(8,128)S(1)}, f32[2,8,512]{2,1,0:T(8,128)S(1)}, f32[8,512]{1,0:T(8,128)S(1)}, f32[8,24,512]{2,1,0:T(8,128)S(1)}, bf16[8,128,512]{...) custom-call(s32[1,1,8]{2,1,0:T(1,128)} %tile_far_ref.1, s32[1,1,8]{2,1,0:T(1,128)} %refs_1_.1, ...), custom_call_target="tpu_custom_call" | custom-call | tf_op jit(solution)/shard_map/spread/pallas_call | solution.py:349
  3.3 23.1 %all_to_all.30 = f32[320,1,128]{2,1,0:T(1,128)S(1)} all-to-all(f32[320,1,128]{2,1,0:T(1,128)S(1)} %bitcast.31), channel_id=1, replica_groups=mesh['gx'=32,'gy'=16] {'gx'}, dimensions={0} | all-to-all | bytes 327680 | tf_op jit(solution)/shard_map/all_to_all | solution.py:363
  26.4 0.0 copy-start
  26.4 1.2 %copy-done = bf16[1024,448]{1,0:T(8,128)(2,1)S(1)} copy-done((bf16[1024,448]{1,0:T(8,128)(2,1)S(1)}, bf16[1024,448]{1,0:T(8,128)(2,1)}, u32[]{:S(2)}) %copy-start) | copy-done | bytes 917528
  27.6 0.0 copy-start.2
  27.6 0.0 copy-start.3
  27.6 0.7 second.1
  28.4 0.0 copy-start.6
  28.4 19.4 %all_to_all.31 = f32[352,1,128]{2,1,0:T(1,128)S(1)} all-to-all(f32[352,1,128]{2,1,0:T(1,128)S(1)} %bitcast.25), channel_id=1, replica_groups=mesh['gx'=32,'gy'=16] {'gy'}, dimensions={0} | all-to-all | bytes 360448 | tf_op jit(solution)/shard_map/all_to_all | solution.py:363
  47.8 0.0 copy-done.2
  47.8 0.0 copy-done.3
  47.8 0.0 copy-done.6
  47.8 0.0 copy-start.1
  47.8 0.7 third.1
  48.5 12.6 %all_to_all.32 = f32[352,1,128]{2,1,0:T(1,128)S(1)} all-to-all(f32[352,1,128]{2,1,0:T(1,128)S(1)} %bitcast.27), channel_id=1, replica_groups=mesh['gx'=32,'gy'=16] {'gy'}, dimensions={0} | all-to-all | bytes 360448 | tf_op jit(solution)/shard_map/all_to_all | solution.py:363
  61.2 0.0 copy-done.1
  61.2 0.0 copy-start.4
  61.2 0.9 fourth.1
  62.1 0.0 copy-start.5
  62.1 13.5 %all_to_all.33 = f32[320,1,128]{2,1,0:T(1,128)S(1)} all-to-all(f32[320,1,128]{2,1,0:T(1,128)S(1)} %bitcast.28), channel_id=1, replica_groups=mesh['gx'=32,'gy'=16] {'gx'}, dimensions={0} | all-to-all | bytes 327680 | tf_op jit(solution)/shard_map/all_to_all | solution.py:363
  75.6 0.0 copy-done.4
  75.6 0.0 copy-done.5
  75.6 1.7 %read.1 = (f32[2,8,512]{2,1,0:T(8,128)S(1)}, f32[32,128]{1,0:T(8,128)S(1)}) custom-call(s32[1,1,8]{2,1,0:T(1,128)} %tile_far_ref.1, f32[320,128]{1,0:T(8,128)S(1)} %bitcast.29, f32[2,1,1,8,512]{4,3,2,1,0:T(8,128)S(1)} %copy-done.5, f32[2,8,512]{2,1,0:T(8,128)S(1)} %get-tuple-element.12.dir_ref, f32[8,512]{1,0:T(8,128)S(1)} %get-tuple-element.13.live_ref, ...), custom_call_target="tpu_custom_call" | custom-call | tf_op jit(solution)/shard_map/read/pallas_call | solution.py:349
  77.2 0.0 copy-start.7
  77.3 12.2 %all_to_all.34 = f32[32,1,128]{2,1,0:T(1,128)S(1)} all-to-all(f32[32,1,128]{2,1,0:T(1,128)S(1)} %bitcast.35), channel_id=1, replica_groups=mesh['gx'=32,'gy'=16] {'gx'}, dimensions={0} | all-to-all | bytes 32768 | tf_op jit(solution)/shard_map/all_to_all | solution.py:363
  89.5 12.0 %all_to_all.35 = f32[16,1,128]{2,1,0:T(1,128)S(1)} all-to-all(f32[16,1,128]{2,1,0:T(1,128)S(1)} %bitcast.34), channel_id=1, replica_groups=mesh['gx'=32,'gy'=16] {'gy'}, dimensions={0} | all-to-all | bytes 16384 | tf_op jit(solution)/shard_map/all_to_all | solution.py:363
  101.5 0.0 copy-done.7
  101.5 0.8 update.1
  (1 shorter events, 0.0 us)
Async XLA Ops:
  26.4 1.2 %copy-start = (bf16[1024,448]{1,0:T(8,128)(2,1)S(1)}, bf16[1024,448]{1,0:T(8,128)(2,1)}, u32[]{:S(2)}) copy-start(bf16[1024,448]{1,0:T(8,128)(2,1)} %constant.13.clone.table_ref) | copy-start | bytes 2752516
  27.6 20.2 %copy-start.2 = (bf16[1024,352]{1,0:T(8,128)(2,1)S(1)}, bf16[1024,352]{1,0:T(8,128)(2,1)}, u32[]{:S(2)}) copy-start(bf16[1024,352]{1,0:T(8,128)(2,1)} %constant.14.clone.table_ref) | copy-start | bytes 2162692
  27.6 20.2 %copy-start.3 = (bf16[704,512]{1,0:T(8,128)(2,1)S(1)}, bf16[704,512]{1,0:T(8,128)(2,1)}, u32[]{:S(2)}) copy-start(bf16[704,512]{1,0:T(8,128)(2,1)} %constant.15.clone.back_ref) | copy-start | bytes 2162692
  28.4 19.5 %copy-start.6 = (f32[8,16,256]{2,1,0:T(8,128)S(1)}, f32[8,16,256]{2,1,0:T(8,128)}, u32[]{:S(2)}) copy-start(f32[8,16,256]{2,1,0:T(8,128)} %spec_ref.1) | copy-start | bytes 393220
  47.8 13.4 %copy-start.1 = (bf16[896,512]{1,0:T(8,128)(2,1)S(1)}, bf16[896,512]{1,0:T(8,128)(2,1)}, u32[]{:S(2)}) copy-start(bf16[896,512]{1,0:T(8,128)(2,1)} %constant.16.clone.table_ref) | copy-start | bytes 2752516
  61.2 14.4 %copy-start.4 = (bf16[512,512]{1,0:T(8,128)(2,1)S(1)}, bf16[512,512]{1,0:T(8,128)(2,1)}, u32[]{:S(2)}) copy-start(bf16[512,512]{1,0:T(8,128)(2,1)} %constant.17.clone.table_ref) | copy-start | bytes 1572868
  62.1 13.5 %copy-start.5 = (f32[2,1,1,8,512]{4,3,2,1,0:T(8,128)S(1)}, f32[2,1,1,8,512]{4,3,2,1,0:T(8,128)}, u32[]{:S(2)}) copy-start(f32[2,1,1,8,512]{4,3,2,1,0:T(8,128)} %res_ref.3) | copy-start | bytes 98308
  77.2 24.2 %copy-start.7 = (f32[2,1,1,8,512]{4,3,2,1,0:T(8,128)S(1)}, f32[2,1,1,8,512]{4,3,2,1,0:T(8,128)}, u32[]{:S(2)}) copy-start(f32[2,1,1,8,512]{4,3,2,1,0:T(8,128)} %iterate_ref.1) | copy-start | bytes 98308

commit v2 on v1

--- a/solution.py
+++ b/solution.py
@@ -202,7 +202,7 @@
 
 def spread_kernel(*refs):
     outside, refs = refs[:6], refs[6:]
-    out_ref, masked_ref, live_ref, depth_ref, plane_high_ref, plane_low_ref, *inside, win_ref, sems = refs
+    out_ref, masked_ref, live_ref, depth_ref, plane_ref, *inside, win_ref, sems = refs
     tile_ref, count_ref, dir_ref, cells_ref, fracs_ref, table_ref = inside
     copies = [pltpu.make_async_copy(far, near, sems.at[at]) for at, (far, near) in enumerate(zip(outside, inside))]
     for copy in copies:
@@ -219,13 +219,12 @@
     weights = point_weights(cells_ref, fracs_ref)
     for slot in range(slots):
         depth, plane = weights(slot)
-        plane_high, plane_low = split(plane)
-        depth_ref[slot], plane_high_ref[slot], plane_low_ref[slot] = depth, plane_high, plane_low
+        planes = jnp.concatenate(split(plane), axis=0)
+        depth_ref[slot], plane_ref[slot] = depth, planes
         values = jnp.concatenate([depth * masked[probe][slot : slot + 1] for probe in range(probes)], axis=0)
-        value_high, value_low = split(values)
         rows = values.shape[0]
-        first = dot(jnp.concatenate([value_high, value_low], axis=0), plane_high, ((1,), (1,)))
-        total = first[:rows] + first[rows:] + dot(value_high, plane_low, ((1,), (1,)))
+        both = dot(jnp.concatenate(split(values), axis=0), planes, ((1,), (1,)))
+        total = both[:rows, :LANES] + (both[:rows, LANES:] + both[rows:, :LANES])
         place = pl.ds(pl.multiple_of(tile_ref[0, 0, slot] * TL, TL), SPAN)
         for probe in range(probes):
             win_ref[probe, place, :] += total[probe * SPAN : (probe + 1) * SPAN]
@@ -272,7 +271,7 @@
 
 
 def read_kernel(
-    tile_far_ref, in_ref, res_ref, dir_ref, live_ref, depth_ref, plane_high_ref, plane_low_ref, table_ref,
+    tile_far_ref, in_ref, res_ref, dir_ref, live_ref, depth_ref, plane_ref, table_ref,
     image_ref, sums_ref, tile_ref, win_ref, sems,
 ):
     copy = pltpu.make_async_copy(tile_far_ref, tile_ref, sems.at[0])
@@ -294,10 +293,11 @@
         place = pl.ds(pl.multiple_of(tile_ref[0, 0, slot] * TL, TL), SPAN)
         block = jnp.concatenate([win_ref[probe, place, :] for probe in range(probes)], axis=0)
         block_high, block_low = split(block)
-        high = plane_high_ref[slot]
         rows = block.shape[0]
-        first = dot(jnp.concatenate([block_high, block_low], axis=0), high)
-        total = first[:rows] + first[rows:] + dot(block_high, plane_low_ref[slot])
+        left = jnp.concatenate([block_high, block_low], axis=0)
+        right = jnp.concatenate([block_high, jnp.zeros_like(block_low)], axis=0)
+        both = dot(jnp.concatenate([left, right], axis=1), plane_ref[slot])
+        total = both[:rows] + both[rows:]
         for probe in range(probes):
             image_ref[probe, slot : slot + 1, :] = jnp.sum(
                 depth_ref[slot] * total[probe * SPAN : (probe + 1) * SPAN], axis=0, keepdims=True
@@ -327,7 +327,9 @@
     out_ref[...] = jnp.broadcast_to(jnp.sum(in_ref[...], axis=0, keepdims=True), out_ref.shape)
 
 
-def update_kernel(sums_ref, image_ref, live_ref, iterate_ref, res_ref, dir_ref, new_iterate_ref, new_res_ref, new_dir_ref):
+def update_kernel(
+    sums_ref, image_ref, live_ref, iterate_ref, res_ref, dir_ref, new_iterate_ref, new_res_ref, new_dir_ref
+):
     sums = jnp.sum(sums_ref[...], axis=0, keepdims=True)
     live = live_ref[...]
     for probe in range(image_ref.shape[0]):
@@ -342,7 +344,7 @@
         new_dir_ref[probe, 0, 0] = new_res + beta * masked_dir
 
 
-def call(kernel, name, outs, operands, far=0, scratch=()):
+def call(kernel, name, outs, operands, far=0, scratch=(), cost=None):
     operands = [pltpu.with_memory_space_constraint(operand, pltpu.HBM) for operand in operands[:far]] + [*operands[far:]]
     near = len(operands) - far
     outs = [jax.ShapeDtypeStruct(*(out if isinstance(out[0], tuple) else (out, f32))) for out in outs]
@@ -353,6 +355,7 @@
         out_specs=[pl.BlockSpec(memory_space=pltpu.VMEM)] * len(outs),
         scratch_shapes=list(scratch),
         compiler_params=pltpu.CompilerParams(vmem_limit_bytes=VMEM_LIMIT),
+        cost_estimate=cost,
         name=name,
     )(*operands)
 
@@ -371,7 +374,7 @@
     near = [
         (pltpu.SMEM if at < 2 else pltpu.VMEM)(operand.shape, operand.dtype) for at, operand in enumerate(operands)
     ]
-    sent, masked, live, depth, plane_high, plane_low = call(
+    sent, masked, live, depth, planes = call(
         spread_kernel,
         "spread",
         [
@@ -379,11 +382,11 @@
             (probes, slots, cap),
             (slots, cap),
             (slots, SPAN, cap),
-            ((slots, LANES, cap), bf16),
-            ((slots, LANES, cap), bf16),
+            ((slots, 2 * LANES, cap), bf16),
         ],
         operands,
         far=len(operands),
+        cost=pl.CostEstimate(flops=400_000_000, bytes_accessed=8_000_000, transcendentals=0),
         scratch=(*near, window, pltpu.SemaphoreType.DMA((len(operands),))),
     )
     came = across("gx", sent)
@@ -397,7 +400,7 @@
         read_kernel,
         "read",
         [(probes, slots, cap), (NX, LANES)],
-        (slot_tile, came, residual, masked, live, depth, plane_high, plane_low, first_back),
+        (slot_tile, came, residual, masked, live, depth, planes, first_back),
         far=1,
         scratch=(near[0], window, pltpu.SemaphoreType.DMA((1,))),
     )

time: 103 us -> 101 us (0.981)
  local copies, waits for them, and re-layouts: 1.26 us -> 0.05 us
    unnamed x16, local copies, waits for them, and re-layouts: 1.26 us -> 0.05 us
where the time goes in v2:
time: 101 us
  blocking collectives  92.9 us (92%)
  Pallas kernels  7.19 us (7%)
    all_to_all x6, blocking collectives, across(): lax.all_to_all(sent, axis, split_axis=0, concat_axis=0, tiled=True)  92.9 us
    pallas_call x7, Pallas kernels, call(): pl.pallas_call(kernel, out_shape=outs, in_specs=[pl.BlockSpec(memory_spac...  7.19 us

profile of v2, /device:TPU:1, one launch (start us, length us, event | category | flops | bytes accessed | tf_op | source)
XLA Modules:
  0.0 100.9 jit_solution(5416983974245215449)
XLA Ops:
  0.6 0.0 copy-start
  0.6 0.0 copy-start.3
  0.7 0.0 copy-start.2
  0.7 0.0 copy-start.6
  0.7 2.8 %spread.1 = (f32[320,128]{1,0:T(8,128)S(1)}, f32[2,8,512]{2,1,0:T(8,128)S(1)}, f32[8,512]{1,0:T(8,128)S(1)}, f32[8,24,512]{2,1,0:T(8,128)S(1)}, bf16[8,256,512]{2,1,0:T(8,128)(2,1)S(1)}) custom-call(s32[1,1,8]{2,1,0:T(1,128)} %tile_far_ref.1, s32[1,1,8]{2,1,0:T(1,128)} %refs_1_.1, f32[2,1,1,8,512]{4,3,2,1,0:T(8,128)} %refs_2_.1, ...), custom_call_target="tpu_custom_call" | custom-call | flops 400000000 | bytes 8000000 | tf_op jit(solution)/shard_map/spread/pallas_call | solution.py:351
  3.4 23.1 %all_to_all.30 = f32[320,1,128]{2,1,0:T(1,128)S(1)} all-to-all(f32[320,1,128]{2,1,0:T(1,128)S(1)} %bitcast.31), channel_id=1, replica_groups=mesh['gx'=32,'gy'=16] {'gx'}, dimensions={0} | all-to-all | bytes 327680 | tf_op jit(solution)/shard_map/all_to_all | solution.py:366
  26.6 0.0 copy-start.1
  26.6 0.0 copy-done
  26.6 0.7 second.1
  27.3 0.0 copy-start.4
  27.3 0.0 copy-start.5
  27.3 19.5 %all_to_all.31 = f32[352,1,128]{2,1,0:T(1,128)S(1)} all-to-all(f32[352,1,128]{2,1,0:T(1,128)S(1)} %bitcast.25), channel_id=1, replica_groups=mesh['gx'=32,'gy'=16] {'gy'}, dimensions={0} | all-to-all | bytes 360448 | tf_op jit(solution)/shard_map/all_to_all | solution.py:366
  46.8 0.0 copy-done.3
  46.8 0.0 copy-done.2
  46.8 0.0 copy-done.6
  46.8 0.7 third.1
  47.5 12.6 %all_to_all.32 = f32[352,1,128]{2,1,0:T(1,128)S(1)} all-to-all(f32[352,1,128]{2,1,0:T(1,128)S(1)} %bitcast.27), channel_id=1, replica_groups=mesh['gx'=32,'gy'=16] {'gy'}, dimensions={0} | all-to-all | bytes 360448 | tf_op jit(solution)/shard_map/all_to_all | solution.py:366
  60.1 0.0 copy-done.1
  60.1 0.9 fourth.1
  61.0 0.0 copy-start.7
  61.0 13.5 %all_to_all.33 = f32[320,1,128]{2,1,0:T(1,128)S(1)} all-to-all(f32[320,1,128]{2,1,0:T(1,128)S(1)} %bitcast.28), channel_id=1, replica_groups=mesh['gx'=32,'gy'=16] {'gx'}, dimensions={0} | all-to-all | bytes 327680 | tf_op jit(solution)/shard_map/all_to_all | solution.py:366
  74.5 0.0 copy-done.4
  74.5 0.0 copy-done.5
  74.5 1.3 %read.1 = (f32[2,8,512]{2,1,0:T(8,128)S(1)}, f32[32,128]{1,0:T(8,128)S(1)}) custom-call(s32[1,1,8]{2,1,0:T(1,128)} %tile_far_ref.1, f32[320,128]{1,0:T(8,128)S(1)} %bitcast.29, f32[2,1,1,8,512]{4,3,2,1,0:T(8,128)S(1)} %copy-done.5, f32[2,8,512]{2,1,0:T(8,128)S(1)} %get-tuple-element.11.dir_ref, f32[8,512]{1,0:T(8,128)S(1)} %get-tuple-element.12.live_ref, ...), custom_call_target="tpu_custom_call" | custom-call | tf_op jit(solution)/shard_map/read/pallas_call | solution.py:351
  75.8 12.2 %all_to_all.34 = f32[32,1,128]{2,1,0:T(1,128)S(1)} all-to-all(f32[32,1,128]{2,1,0:T(1,128)S(1)} %bitcast.35), channel_id=1, replica_groups=mesh['gx'=32,'gy'=16] {'gx'}, dimensions={0} | all-to-all | bytes 32768 | tf_op jit(solution)/shard_map/all_to_all | solution.py:366
  88.0 12.0 %all_to_all.35 = f32[16,1,128]{2,1,0:T(1,128)S(1)} all-to-all(f32[16,1,128]{2,1,0:T(1,128)S(1)} %bitcast.34), channel_id=1, replica_groups=mesh['gx'=32,'gy'=16] {'gy'}, dimensions={0} | all-to-all | bytes 16384 | tf_op jit(solution)/shard_map/all_to_all | solution.py:366
  100.1 0.0 copy-done.7
  100.1 0.8 update.1
  (1 shorter events, 0.0 us)
Async XLA Ops:
  0.6 25.9 %copy-start = (bf16[1024,448]{1,0:T(8,128)(2,1)S(1)}, bf16[1024,448]{1,0:T(8,128)(2,1)}, u32[]{:S(2)}) copy-start(bf16[1024,448]{1,0:T(8,128)(2,1)} %constant.13.clone.table_ref) | copy-start | bytes 2752516
  0.6 46.1 %copy-start.3 = (bf16[704,512]{1,0:T(8,128)(2,1)S(1)}, bf16[704,512]{1,0:T(8,128)(2,1)}, u32[]{:S(2)}) copy-start(bf16[704,512]{1,0:T(8,128)(2,1)} %constant.15.clone.back_ref) | copy-start | bytes 2162692
  0.7 46.1 %copy-start.2 = (bf16[1024,352]{1,0:T(8,128)(2,1)S(1)}, bf16[1024,352]{1,0:T(8,128)(2,1)}, u32[]{:S(2)}) copy-start(bf16[1024,352]{1,0:T(8,128)(2,1)} %constant.14.clone.table_ref) | copy-start | bytes 2162692
  0.7 46.1 %copy-start.6 = (f32[8,16,256]{2,1,0:T(8,128)S(1)}, f32[8,16,256]{2,1,0:T(8,128)}, u32[]{:S(2)}) copy-start(f32[8,16,256]{2,1,0:T(8,128)} %spec_ref.1) | copy-start | bytes 393220
  26.6 33.6 %copy-start.1 = (bf16[896,512]{1,0:T(8,128)(2,1)S(1)}, bf16[896,512]{1,0:T(8,128)(2,1)}, u32[]{:S(2)}) copy-start(bf16[896,512]{1,0:T(8,128)(2,1)} %constant.16.clone.table_ref) | copy-start | bytes 2752516
  27.3 47.2 %copy-start.4 = (bf16[512,512]{1,0:T(8,128)(2,1)S(1)}, bf16[512,512]{1,0:T(8,128)(2,1)}, u32[]{:S(2)}) copy-start(bf16[512,512]{1,0:T(8,128)(2,1)} %constant.17.clone.table_ref) | copy-start | bytes 1572868
  27.3 47.2 %copy-start.5 = (f32[2,1,1,8,512]{4,3,2,1,0:T(8,128)S(1)}, f32[2,1,1,8,512]{4,3,2,1,0:T(8,128)}, u32[]{:S(2)}) copy-start(f32[2,1,1,8,512]{4,3,2,1,0:T(8,128)} %res_ref.3) | copy-start | bytes 98308
  61.0 39.0 %copy-start.7 = (f32[2,1,1,8,512]{4,3,2,1,0:T(8,128)S(1)}, f32[2,1,1,8,512]{4,3,2,1,0:T(8,128)}, u32[]{:S(2)}) copy-start(f32[2,1,1,8,512]{4,3,2,1,0:T(8,128)} %iterate_ref.1) | copy-start | bytes 98308

commit v3 on v2

--- a/solution.py
+++ b/solution.py
@@ -43,15 +43,12 @@
     return np.cos(angle) * scale, sign * np.sin(angle) * scale
 
 
-def complex_table(out_index, out_part, out_ok, in_index, in_part, in_ok, sign, scale):
-    real, imag = rotation(out_index, in_index, sign, scale)
-    same = out_part[:, None] == in_part[None, :]
-    crossed = np.where(out_part[:, None] == 1, imag, -imag)
-    table = np.where(same, real, crossed)
-    table = np.where(out_ok[:, None] & in_ok[None, :], table, 0.0)
-    high = table.astype(ml_dtypes.bfloat16)
-    low = (table - high.astype(np.float64)).astype(ml_dtypes.bfloat16)
-    return np.concatenate([high, low], axis=0)
+def table(out_index, out_ok, in_index, in_ok, sign, scale):
+    parts = rotation(out_index, in_index, sign, scale)
+    values = np.concatenate([np.where(out_ok[:, None] & in_ok[None, :], part, 0.0) for part in parts], axis=0)
+    high = values.astype(ml_dtypes.bfloat16)
+    low = (values - high.astype(np.float64)).astype(ml_dtypes.bfloat16)
+    return np.concatenate([high, low, high], axis=1)
 
 
 def window_index(owner, offset, wide):
@@ -65,29 +62,23 @@
         return [part.reshape(-1) for part in np.meshgrid(*[np.arange(size) for size in sizes], indexing="ij")]
 
     yes = lambda rows: np.ones(rows.shape, bool)
-    n1_part, n1 = grid(2, G)
-    k1_part, k1_low, k1_owner = grid(2, K_ONE, NX)
+    n1 = np.arange(G)
+    k1_low, k1_owner = grid(K_ONE, NX)
     k1 = k1_owner * K_ONE + k1_low
-    x_part, x_cell, x_owner = grid(2, WIN_ONE, NX)
+    x_cell, x_owner = grid(WIN_ONE, NX)
     n2, n2_ok = window_index(x_owner, x_cell, WIDE_ONE)
-    came = np.concatenate(
-        [
-            (np.arange(NX)[:, None] + NX * np.arange(ROWS_X)[None, :]).reshape(-1),
-            np.arange(NX * ROWS_X, NX * PARTS_X),
-        ]
-    )
-    k2_part, k2_low, k2_owner = grid(2, K_TWO, NY)
+    k2_low, k2_owner = grid(K_TWO, NY)
     k2 = k2_owner * K_TWO + k2_low
-    y_owner, y_cell, y_part = grid(NY, WIN_TWO, 2)
+    y_cell, y_owner = grid(WIN_TWO, NY)
     n3, n3_ok = window_index(y_owner, y_cell, WIDE_TWO)
-    k3_part, k3 = grid(2, LENGTH)
+    k3 = np.arange(LENGTH)
     return (
-        complex_table(k1, k1_part, yes(k1), n1, n1_part, yes(n1), -1.0, 1.0),
-        complex_table(k2, k2_part, yes(k2), n2[came], x_part[came], n2_ok[came], -1.0, 1.0),
-        complex_table(k3, k3_part, yes(k3), n3, y_part, n3_ok, -1.0, 1.0),
-        complex_table(n3, y_part, n3_ok, k3, k3_part, yes(k3), 1.0, 1.0 / LENGTH),
-        complex_table(n2, x_part, n2_ok, k2, k2_part, yes(k2), 1.0, 1.0 / LENGTH),
-        complex_table(n1, n1_part, yes(n1), k1, k1_part, yes(k1), 1.0, 1.0 / LENGTH),
+        table(k1, yes(k1), n1, yes(n1), -1.0, 1.0),
+        table(k2, yes(k2), n2, n2_ok, -1.0, 1.0),
+        table(k3, yes(k3), n3, n3_ok, -1.0, 1.0),
+        table(n3, n3_ok, k3, yes(k3), 1.0, 1.0 / LENGTH),
+        table(n2, n2_ok, k2, yes(k2), 1.0, 1.0 / LENGTH),
+        table(n1, yes(n1), k1, yes(k1), 1.0, 1.0 / LENGTH),
     )
 
 
@@ -100,11 +91,12 @@
     return lax.dot_general(left, right, (dims, ((), ())), preferred_element_type=f32)
 
 
-def transform(table_ref, data):
+def transform(table_ref, real, imag):
+    high, low = split(jnp.concatenate([real, imag], axis=1))
+    data = jnp.concatenate([high, high, low], axis=0)
     rows = table_ref.shape[0] // 2
-    data_high, data_low = split(data)
-    both = dot(table_ref[:rows], jnp.concatenate([data_high, data_low], axis=1))
-    return both[:, :LANES] + both[:, LANES:] + dot(table_ref[rows:], data_high)
+    cos, sin = dot(table_ref[:rows], data), dot(table_ref[rows:], data)
+    return cos[:, :LANES] - sin[:, LANES:], cos[:, LANES:] + sin[:, :LANES]
 
 
 def exchange(arrays, block):
@@ -228,34 +220,40 @@
         place = pl.ds(pl.multiple_of(tile_ref[0, 0, slot] * TL, TL), SPAN)
         for probe in range(probes):
             win_ref[probe, place, :] += total[probe * SPAN : (probe + 1) * SPAN]
-    field = jnp.concatenate([win_ref[0, 1 : G + 1, :], win_ref[1, 1 : G + 1, :]], axis=0)
     for copy in copies[5:]:
         copy.wait()
-    columns = transform(table_ref, field)
     rows = []
-    for part in range(2):
-        start = part * LENGTH
-        pieces = [columns[start + low * NX : start + (low + 1) * NX] for low in range(K_ONE)]
+    for columns in transform(table_ref, win_ref[0, 1 : G + 1, :], win_ref[1, 1 : G + 1, :]):
+        pieces = [columns[low * NX : (low + 1) * NX] for low in range(K_ONE)]
         rows += exchange(pieces, PAD_TWO)[:WIN_ONE]
     for row, piece in enumerate(pack(rows)):
         out_ref[pl.ds(row, NX, stride=ROWS_X), :] = piece
 
 
+def window_rows(in_ref):
+    rows = [gather(in_ref, row, NX, ROWS_X) for row in range(ROWS_X)]
+    return rows + unpack(rows)
+
+
 def second_kernel(in_ref, table_ref, out_ref):
-    extra = unpack([gather(in_ref, row, NX, ROWS_X) for row in range(2 * EXTRA_X + 1)])
-    columns = transform(table_ref, jnp.concatenate([in_ref[...], *extra], axis=0))
-    for part in range(2):
-        start = part * LENGTH
-        pieces = [columns[start + low * NY : start + (low + 1) * NY] for low in range(K_TWO)]
+    rows = window_rows(in_ref)
+    window = [jnp.concatenate(rows[part * WIN_ONE : (part + 1) * WIN_ONE], axis=0) for part in range(2)]
+    for part, columns in enumerate(transform(table_ref, *window)):
+        pieces = [columns[low * NY : (low + 1) * NY] for low in range(K_TWO)]
         for cell, piece in enumerate(exchange(pieces, 1)[:WIN_TWO]):
             out_ref[pl.ds(2 * cell + part, NY, stride=ROWS_Y), :] = piece
 
 
 def third_kernel(in_ref, spec_ref, table_ref, back_ref, out_ref):
-    columns = transform(table_ref, in_ref[...])
+    window = [
+        jnp.concatenate([gather(in_ref, 2 * cell + part, NY, ROWS_Y) for cell in range(WIN_TWO)], axis=0)
+        for part in range(2)
+    ]
     factor = spec_ref[...].reshape(LANES, LENGTH).T
-    scaled = jnp.concatenate([columns[:LENGTH] * factor, columns[LENGTH:] * factor], axis=0)
-    out_ref[...] = transform(back_ref, scaled)
+    scaled = [columns * factor for columns in transform(table_ref, *window)]
+    for part, columns in enumerate(transform(back_ref, *scaled)):
+        for cell in range(WIN_TWO):
+            out_ref[pl.ds(2 * cell + part, NY, stride=ROWS_Y), :] = columns[cell * NY : (cell + 1) * NY]
 
 
 def fourth_kernel(in_ref, table_ref, out_ref):
@@ -263,9 +261,10 @@
     for part in range(2):
         pieces = [gather(in_ref, 2 * cell + part, NY, ROWS_Y) for cell in range(WIN_TWO)]
         pieces += [jnp.zeros((NY, LANES), f32)] * (K_TWO - WIN_TWO)
-        parts += exchange(pieces, 1)
-    columns = transform(table_ref, jnp.concatenate(parts, axis=0))
-    rows = [columns[row * NX : (row + 1) * NX] for row in range(PARTS_X)]
+        parts.append(jnp.concatenate(exchange(pieces, 1), axis=0))
+    rows = []
+    for columns in transform(table_ref, *parts):
+        rows += [columns[cell * NX : (cell + 1) * NX] for cell in range(WIN_ONE)]
     for row, piece in enumerate(pack(rows)):
         out_ref[pl.ds(row, NX, stride=ROWS_X), :] = piece
 
@@ -277,17 +276,16 @@
     copy = pltpu.make_async_copy(tile_far_ref, tile_ref, sems.at[0])
     copy.start()
     probes, slots = image_ref.shape[:2]
-    rows = [gather(in_ref, row, NX, ROWS_X) for row in range(ROWS_X)]
-    rows += unpack(rows)
+    rows = window_rows(in_ref)
     parts = []
     for part in range(2):
         pieces = rows[part * WIN_ONE : (part + 1) * WIN_ONE]
         pieces += [jnp.zeros((NX, LANES), f32)] * (PAD_ONE - WIN_ONE)
-        parts += exchange(pieces, PAD_TWO)
-    smooth = transform(table_ref, jnp.concatenate(parts, axis=0))
+        parts.append(jnp.concatenate(exchange(pieces, PAD_TWO), axis=0))
+    smooth = transform(table_ref, *parts)
     win_ref[...] = jnp.zeros_like(win_ref)
     for probe in range(probes):
-        win_ref[probe, 1 : G + 1, :] = smooth[probe * G : (probe + 1) * G]
+        win_ref[probe, 1 : G + 1, :] = smooth[probe]
     copy.wait()
     for slot in range(slots):
         place = pl.ds(pl.multiple_of(tile_ref[0, 0, slot] * TL, TL), SPAN)

time: 101 us -> 101 us (level)
  no operation moved by 1% of the time
where the time goes in v3:
time: 101 us
  blocking collectives  93.1 us (92%)
  Pallas kernels  6.97 us (7%)
    all_to_all x6, blocking collectives, across(): lax.all_to_all(sent, axis, split_axis=0, concat_axis=0, tiled=True)  93.1 us
    pallas_call x7, Pallas kernels, call(): pl.pallas_call(kernel, out_shape=outs, in_specs=[pl.BlockSpec(memory_spac...  6.97 us

profile of v3, /device:TPU:1, one launch (start us, length us, event | category | flops | bytes accessed | tf_op | source)
XLA Modules:
  0.0 100.8 jit_solution(9425394994148674713)
XLA Ops:
  0.6 0.0 copy-start
  0.6 0.0 copy-start.3
  0.7 0.0 copy-start.2
  0.7 0.0 copy-start.5
  0.7 2.7 %spread.1 = (f32[320,128]{1,0:T(8,128)S(1)}, f32[2,8,512]{2,1,0:T(8,128)S(1)}, f32[8,512]{1,0:T(8,128)S(1)}, f32[8,24,512]{2,1,0:T(8,128)S(1)}, bf16[8,256,512]{2,1,0:T(8,128)(2,1)S(1)}) custom-call(s32[1,1,8]{2,1,0:T(1,128)} %tile_far_ref.1, s32[1,1,8]{2,1,0:T(1,128)} %refs_1_.1, f32[2,1,1,8,512]{4,3,2,1,0:T(8,128)} %refs_2_.1, ...), custom_call_target="tpu_custom_call" | custom-call | flops 400000000 | bytes 8000000 | tf_op jit(solution)/shard_map/spread/pallas_call | solution.py:349
  3.4 0.0 copy-start.1
  3.4 23.3 %all_to_all.30 = f32[320,1,128]{2,1,0:T(1,128)S(1)} all-to-all(f32[320,1,128]{2,1,0:T(1,128)S(1)} %bitcast.31), channel_id=1, replica_groups=mesh['gx'=32,'gy'=16] {'gx'}, dimensions={0} | all-to-all | bytes 327680 | tf_op jit(solution)/shard_map/all_to_all | solution.py:364
  26.7 0.0 copy-done
  26.7 0.7 second.1
  27.4 0.0 copy-start.4
  27.5 0.0 copy-start.6
  27.5 19.5 %all_to_all.31 = f32[352,1,128]{2,1,0:T(1,128)S(1)} all-to-all(f32[352,1,128]{2,1,0:T(1,128)S(1)} %bitcast.26), channel_id=1, replica_groups=mesh['gx'=32,'gy'=16] {'gy'}, dimensions={0} | all-to-all | bytes 360448 | tf_op jit(solution)/shard_map/all_to_all | solution.py:364
  46.9 0.0 copy-done.3
  46.9 0.0 copy-done.2
  46.9 0.0 copy-done.5
  46.9 0.6 third.1
  47.6 12.6 %all_to_all.32 = f32[352,1,128]{2,1,0:T(1,128)S(1)} all-to-all(f32[352,1,128]{2,1,0:T(1,128)S(1)} %bitcast.25), channel_id=1, replica_groups=mesh['gx'=32,'gy'=16] {'gy'}, dimensions={0} | all-to-all | bytes 360448 | tf_op jit(solution)/shard_map/all_to_all | solution.py:364
  60.2 0.0 copy-done.1
  60.2 0.0 copy-start.7
  60.2 0.7 fourth.1
  61.0 13.5 %all_to_all.33 = f32[320,1,128]{2,1,0:T(1,128)S(1)} all-to-all(f32[320,1,128]{2,1,0:T(1,128)S(1)} %bitcast.29), channel_id=1, replica_groups=mesh['gx'=32,'gy'=16] {'gx'}, dimensions={0} | all-to-all | bytes 327680 | tf_op jit(solution)/shard_map/all_to_all | solution.py:364
  74.5 0.0 copy-done.4
  74.5 0.0 copy-done.6
  74.5 1.3 %read.1 = (f32[2,8,512]{2,1,0:T(8,128)S(1)}, f32[32,128]{1,0:T(8,128)S(1)}) custom-call(s32[1,1,8]{2,1,0:T(1,128)} %tile_far_ref.1, f32[320,128]{1,0:T(8,128)S(1)} %bitcast.30, f32[2,1,1,8,512]{4,3,2,1,0:T(8,128)S(1)} %copy-done.6, f32[2,8,512]{2,1,0:T(8,128)S(1)} %get-tuple-element.11.dir_ref, f32[8,512]{1,0:T(8,128)S(1)} %get-tuple-element.12.live_ref, ...), custom_call_target="tpu_custom_call" | custom-call | tf_op jit(solution)/shard_map/read/pallas_call | solution.py:349
  75.7 12.2 %all_to_all.34 = f32[32,1,128]{2,1,0:T(1,128)S(1)} all-to-all(f32[32,1,128]{2,1,0:T(1,128)S(1)} %bitcast.35), channel_id=1, replica_groups=mesh['gx'=32,'gy'=16] {'gx'}, dimensions={0} | all-to-all | bytes 32768 | tf_op jit(solution)/shard_map/all_to_all | solution.py:364
  87.9 12.0 %all_to_all.35 = f32[16,1,128]{2,1,0:T(1,128)S(1)} all-to-all(f32[16,1,128]{2,1,0:T(1,128)S(1)} %bitcast.34), channel_id=1, replica_groups=mesh['gx'=32,'gy'=16] {'gy'}, dimensions={0} | all-to-all | bytes 16384 | tf_op jit(solution)/shard_map/all_to_all | solution.py:364
  100.0 0.0 copy-done.7
  100.0 0.8 update.1
  (1 shorter events, 0.0 us)
Async XLA Ops:
  0.6 26.1 %copy-start = (bf16[512,672]{1,0:T(8,128)(2,1)S(1)}, bf16[512,672]{1,0:T(8,128)(2,1)}, u32[]{:S(2)}) copy-start(bf16[512,672]{1,0:T(8,128)(2,1)} %constant.13.clone.table_ref) | copy-start | bytes 2064388
  0.6 46.3 %copy-start.3 = (bf16[352,768]{1,0:T(8,128)(2,1)S(1)}, bf16[352,768]{1,0:T(8,128)(2,1)}, u32[]{:S(2)}) copy-start(bf16[352,768]{1,0:T(8,128)(2,1)} %constant.15.clone.back_ref) | copy-start | bytes 1622020
  0.7 46.3 %copy-start.2 = (bf16[512,528]{1,0:T(8,128)(2,1)S(1)}, bf16[512,528]{1,0:T(8,128)(2,1)}, u32[]{:S(2)}) copy-start(bf16[512,528]{1,0:T(8,128)(2,1)} %constant.14.clone.table_ref) | copy-start | bytes 1622020
  0.7 46.3 %copy-start.5 = (f32[8,16,256]{2,1,0:T(8,128)S(1)}, f32[8,16,256]{2,1,0:T(8,128)}, u32[]{:S(2)}) copy-start(f32[8,16,256]{2,1,0:T(8,128)} %spec_ref.1) | copy-start | bytes 393220
  3.4 56.8 %copy-start.1 = (bf16[448,768]{1,0:T(8,128)(2,1)S(1)}, bf16[448,768]{1,0:T(8,128)(2,1)}, u32[]{:S(2)}) copy-start(bf16[448,768]{1,0:T(8,128)(2,1)} %constant.16.clone.table_ref) | copy-start | bytes 2064388
  27.4 47.0 %copy-start.4 = (bf16[256,768]{1,0:T(8,128)(2,1)S(1)}, bf16[256,768]{1,0:T(8,128)(2,1)}, u32[]{:S(2)}) copy-start(bf16[256,768]{1,0:T(8,128)(2,1)} %constant.17.clone.table_ref) | copy-start | bytes 1179652
  27.5 47.0 %copy-start.6 = (f32[2,1,1,8,512]{4,3,2,1,0:T(8,128)S(1)}, f32[2,1,1,8,512]{4,3,2,1,0:T(8,128)}, u32[]{:S(2)}) copy-start(f32[2,1,1,8,512]{4,3,2,1,0:T(8,128)} %res_ref.3) | copy-start | bytes 98308
  60.2 39.8 %copy-start.7 = (f32[2,1,1,8,512]{4,3,2,1,0:T(8,128)S(1)}, f32[2,1,1,8,512]{4,3,2,1,0:T(8,128)}, u32[]{:S(2)}) copy-start(f32[2,1,1,8,512]{4,3,2,1,0:T(8,128)} %iterate_ref.1) | copy-start | bytes 98308

commit v4 on v3

--- a/solution.py
+++ b/solution.py
@@ -397,14 +397,14 @@
     image, sums = call(
         read_kernel,
         "read",
-        [(probes, slots, cap), (NX, LANES)],
+        [(probes, slots, cap), (NY, LANES)],
         (slot_tile, came, residual, masked, live, depth, planes, first_back),
         far=1,
         scratch=(near[0], window, pltpu.SemaphoreType.DMA((1,))),
     )
+    sums = across("gy", sums)
+    (sums,) = call(total_kernel, "total", [(NX, LANES)], (sums,))
     sums = across("gx", sums)
-    (sums,) = call(total_kernel, "total", [(NY, LANES)], (sums,))
-    sums = across("gy", sums)
     return tuple(call(update_kernel, "update", [direction.shape] * 3, (sums, image, live, iterate, residual, masked)))
 
 

time: 101 us -> 99.7 us (0.987)
  blocking collectives: 93.1 us -> 91.6 us
    all_to_all x6, blocking collectives: 93.1 us -> 91.6 us  [across(): lax.all_to_all(sent, axis, split_axis=0, concat_axis=0, tiled=True)]
where the time goes in v4:
time: 99.7 us; the launch traced here: 99.4 us
  blocking collectives  91.6 us (92%)
  Pallas kernels  6.98 us (7%)
    all_to_all x6, blocking collectives, across(): lax.all_to_all(sent, axis, split_axis=0, concat_axis=0, tiled=True)  91.6 us
    pallas_call x7, Pallas kernels, call(): pl.pallas_call(kernel, out_shape=outs, in_specs=[pl.BlockSpec(memory_spac...  6.98 us

profile of v4, /device:TPU:1, one launch (start us, length us, event | category | flops | bytes accessed | tf_op | source)
XLA Modules:
  0.0 99.4 jit_solution(16436655241411373405)
XLA Ops:
  0.6 0.0 copy-start
  0.6 0.0 copy-start.3
  0.7 0.0 copy-start.2
  0.7 0.0 copy-start.5
  0.7 2.7 %spread.1 = (f32[320,128]{1,0:T(8,128)S(1)}, f32[2,8,512]{2,1,0:T(8,128)S(1)}, f32[8,512]{1,0:T(8,128)S(1)}, f32[8,24,512]{2,1,0:T(8,128)S(1)}, bf16[8,256,512]{2,1,0:T(8,128)(2,1)S(1)}) custom-call(s32[1,1,8]{2,1,0:T(1,128)} %tile_far_ref.1, s32[1,1,8]{2,1,0:T(1,128)} %refs_1_.1, f32[2,1,1,8,512]{4,3,2,1,0:T(8,128)} %refs_2_.1, ...), custom_call_target="tpu_custom_call" | custom-call | flops 400000000 | bytes 8000000 | tf_op jit(solution)/shard_map/spread/pallas_call | solution.py:349
  3.4 0.0 copy-start.1
  3.4 23.3 %all_to_all.30 = f32[320,1,128]{2,1,0:T(1,128)S(1)} all-to-all(f32[320,1,128]{2,1,0:T(1,128)S(1)} %bitcast.31), channel_id=1, replica_groups=mesh['gx'=32,'gy'=16] {'gx'}, dimensions={0} | all-to-all | bytes 327680 | tf_op jit(solution)/shard_map/all_to_all | solution.py:364
  26.7 0.0 copy-done
  26.7 0.7 second.1
  27.5 0.0 copy-start.4
  27.5 0.0 copy-start.6
  27.5 19.5 %all_to_all.31 = f32[352,1,128]{2,1,0:T(1,128)S(1)} all-to-all(f32[352,1,128]{2,1,0:T(1,128)S(1)} %bitcast.26), channel_id=1, replica_groups=mesh['gx'=32,'gy'=16] {'gy'}, dimensions={0} | all-to-all | bytes 360448 | tf_op jit(solution)/shard_map/all_to_all | solution.py:364
  46.9 0.0 copy-done.3
  46.9 0.0 copy-done.2
  46.9 0.0 copy-done.5
  46.9 0.6 third.1
  47.6 12.6 %all_to_all.32 = f32[352,1,128]{2,1,0:T(1,128)S(1)} all-to-all(f32[352,1,128]{2,1,0:T(1,128)S(1)} %bitcast.25), channel_id=1, replica_groups=mesh['gx'=32,'gy'=16] {'gy'}, dimensions={0} | all-to-all | bytes 360448 | tf_op jit(solution)/shard_map/all_to_all | solution.py:364
  60.2 0.0 copy-done.1
  60.2 0.0 copy-start.7
  60.2 0.7 fourth.1
  61.0 13.5 %all_to_all.33 = f32[320,1,128]{2,1,0:T(1,128)S(1)} all-to-all(f32[320,1,128]{2,1,0:T(1,128)S(1)} %bitcast.29), channel_id=1, replica_groups=mesh['gx'=32,'gy'=16] {'gx'}, dimensions={0} | all-to-all | bytes 327680 | tf_op jit(solution)/shard_map/all_to_all | solution.py:364
  74.5 0.0 copy-done.4
  74.5 0.0 copy-done.6
  74.5 1.3 %read.1 = (f32[2,8,512]{2,1,0:T(8,128)S(1)}, f32[16,128]{1,0:T(8,128)S(1)}) custom-call(s32[1,1,8]{2,1,0:T(1,128)} %tile_far_ref.1, f32[320,128]{1,0:T(8,128)S(1)} %bitcast.30, f32[2,1,1,8,512]{4,3,2,1,0:T(8,128)S(1)} %copy-done.6, f32[2,8,512]{2,1,0:T(8,128)S(1)} %get-tuple-element.11.dir_ref, f32[8,512]{1,0:T(8,128)S(1)} %get-tuple-element.12.live_ref, ...), custom_call_target="tpu_custom_call" | custom-call | tf_op jit(solution)/shard_map/read/pallas_call | solution.py:349
  75.8 11.2 %all_to_all.34 = f32[16,1,128]{2,1,0:T(1,128)S(1)} all-to-all(f32[16,1,128]{2,1,0:T(1,128)S(1)} %bitcast.35), channel_id=1, replica_groups=mesh['gx'=32,'gy'=16] {'gy'}, dimensions={0} | all-to-all | bytes 16384 | tf_op jit(solution)/shard_map/all_to_all | solution.py:364
  86.9 11.6 %all_to_all.35 = f32[32,1,128]{2,1,0:T(1,128)S(1)} all-to-all(f32[32,1,128]{2,1,0:T(1,128)S(1)} %bitcast.33), channel_id=1, replica_groups=mesh['gx'=32,'gy'=16] {'gx'}, dimensions={0} | all-to-all | bytes 32768 | tf_op jit(solution)/shard_map/all_to_all | solution.py:364
  98.6 0.0 copy-done.7
  98.6 0.8 update.1
  (1 shorter events, 0.0 us)
Async XLA Ops:
  0.6 26.1 %copy-start = (bf16[512,672]{1,0:T(8,128)(2,1)S(1)}, bf16[512,672]{1,0:T(8,128)(2,1)}, u32[]{:S(2)}) copy-start(bf16[512,672]{1,0:T(8,128)(2,1)} %constant.13.clone.table_ref) | copy-start | bytes 2064388
  0.6 46.3 %copy-start.3 = (bf16[352,768]{1,0:T(8,128)(2,1)S(1)}, bf16[352,768]{1,0:T(8,128)(2,1)}, u32[]{:S(2)}) copy-start(bf16[352,768]{1,0:T(8,128)(2,1)} %constant.15.clone.back_ref) | copy-start | bytes 1622020
  0.7 46.3 %copy-start.2 = (bf16[512,528]{1,0:T(8,128)(2,1)S(1)}, bf16[512,528]{1,0:T(8,128)(2,1)}, u32[]{:S(2)}) copy-start(bf16[512,528]{1,0:T(8,128)(2,1)} %constant.14.clone.table_ref) | copy-start | bytes 1622020
  0.7 46.3 %copy-start.5 = (f32[8,16,256]{2,1,0:T(8,128)S(1)}, f32[8,16,256]{2,1,0:T(8,128)}, u32[]{:S(2)}) copy-start(f32[8,16,256]{2,1,0:T(8,128)} %spec_ref.1) | copy-start | bytes 393220
  3.4 56.8 %copy-start.1 = (bf16[448,768]{1,0:T(8,128)(2,1)S(1)}, bf16[448,768]{1,0:T(8,128)(2,1)}, u32[]{:S(2)}) copy-start(bf16[448,768]{1,0:T(8,128)(2,1)} %constant.16.clone.table_ref) | copy-start | bytes 2064388
  27.5 47.0 %copy-start.4 = (bf16[256,768]{1,0:T(8,128)(2,1)S(1)}, bf16[256,768]{1,0:T(8,128)(2,1)}, u32[]{:S(2)}) copy-start(bf16[256,768]{1,0:T(8,128)(2,1)} %constant.17.clone.table_ref) | copy-start | bytes 1179652
  27.5 47.0 %copy-start.6 = (f32[2,1,1,8,512]{4,3,2,1,0:T(8,128)S(1)}, f32[2,1,1,8,512]{4,3,2,1,0:T(8,128)}, u32[]{:S(2)}) copy-start(f32[2,1,1,8,512]{4,3,2,1,0:T(8,128)} %res_ref.3) | copy-start | bytes 98308
  60.2 38.3 %copy-start.7 = (f32[2,1,1,8,512]{4,3,2,1,0:T(8,128)S(1)}, f32[2,1,1,8,512]{4,3,2,1,0:T(8,128)}, u32[]{:S(2)}) copy-start(f32[2,1,1,8,512]{4,3,2,1,0:T(8,128)} %iterate_ref.1) | copy-start | bytes 98308

commit v5 on v4

--- a/solution.py
+++ b/solution.py
@@ -56,6 +56,10 @@
     return cell, (cell >= 0) & (cell < G)
 
 
+def cells_of(window, parity):
+    return list(range(1 - parity, window, 2))
+
+
 @functools.lru_cache(None)
 def tables():
     def grid(*sizes):
@@ -65,21 +69,22 @@
     n1 = np.arange(G)
     k1_low, k1_owner = grid(K_ONE, NX)
     k1 = k1_owner * K_ONE + k1_low
-    x_cell, x_owner = grid(WIN_ONE, NX)
-    n2, n2_ok = window_index(x_owner, x_cell, WIDE_ONE)
-    k2_low, k2_owner = grid(K_TWO, NY)
+    first = table(k1, yes(k1), n1, yes(n1), -1.0, 1.0)
+    first_back = table(n1, yes(n1), k1, yes(k1), 1.0, 1.0 / LENGTH)
+    k2_low, k2_owner = grid(K_TWO, NY // 2)
     k2 = k2_owner * K_TWO + k2_low
-    y_cell, y_owner = grid(WIN_TWO, NY)
-    n3, n3_ok = window_index(y_owner, y_cell, WIDE_TWO)
-    k3 = np.arange(LENGTH)
-    return (
-        table(k1, yes(k1), n1, yes(n1), -1.0, 1.0),
-        table(k2, yes(k2), n2, n2_ok, -1.0, 1.0),
-        table(k3, yes(k3), n3, n3_ok, -1.0, 1.0),
-        table(n3, n3_ok, k3, yes(k3), 1.0, 1.0 / LENGTH),
-        table(n2, n2_ok, k2, yes(k2), 1.0, 1.0 / LENGTH),
-        table(n1, yes(n1), k1, yes(k1), 1.0, 1.0 / LENGTH),
-    )
+    k3 = np.arange(LENGTH // 2)
+    wholes = []
+    for k, window, owners, wide in ((k2, WIN_ONE, NX, WIDE_ONE), (k3, WIN_TWO, NY, WIDE_TWO)):
+        out, back = [], []
+        for parity in range(2):
+            cell, owner = grid(len(cells_of(window, parity)), owners)
+            n, n_ok = window_index(owner, 2 * cell + 1 - parity, wide)
+            out.append(table(k, yes(k), n, n_ok, -1.0, 1.0))
+            back.append(table(n, n_ok, k, yes(k), 1.0, 1.0 / LENGTH))
+        gap = np.zeros((out[1].shape[0], -out[1].shape[1] % LANES), ml_dtypes.bfloat16)
+        wholes.append((np.concatenate([out[1], gap, out[0]], axis=1), np.concatenate(back, axis=0)))
+    return first, wholes[0][0], wholes[1][0], wholes[1][1], wholes[0][1], first_back
 
 
 def split(value):
@@ -91,12 +96,52 @@
     return lax.dot_general(left, right, (dims, ((), ())), preferred_element_type=f32)
 
 
-def transform(table_ref, real, imag):
+def transform(table, real, imag):
     high, low = split(jnp.concatenate([real, imag], axis=1))
     data = jnp.concatenate([high, high, low], axis=0)
-    rows = table_ref.shape[0] // 2
-    cos, sin = dot(table_ref[:rows], data), dot(table_ref[rows:], data)
+    rows = table.shape[0] // 2
+    cos, sin = dot(table[:rows], data), dot(table[rows:], data)
     return cos[:, :LANES] - sin[:, LANES:], cos[:, LANES:] + sin[:, :LANES]
+
+
+def transform_window(table_ref, parts, owners):
+    results = []
+    for parity in range(2):
+        places = cells_of(len(parts[0]), parity)
+        depth = 3 * len(places) * owners
+        start = 0 if parity else table_ref.shape[1] - depth
+        data = [jnp.concatenate([rows[place] for place in places], axis=0) for rows in parts]
+        results.append(transform(table_ref[:, start : start + depth], *data))
+    return [(even + odd, even - odd) for even, odd in zip(*results)]
+
+
+def window_transform(table_ref, parts, window, owners):
+    rows = [[None] * window for _ in parts]
+    start = 0
+    for parity in range(2):
+        places = cells_of(window, parity)
+        data = [low - high if parity else low + high for low, high in parts]
+        end = start + 2 * len(places) * owners
+        for part, columns in enumerate(transform(table_ref[start:end], *data)):
+            for at, place in enumerate(places):
+                rows[part][place] = columns[at * owners : (at + 1) * owners]
+        start = end
+    return rows
+
+
+def exchange_turned(arrays, block, count):
+    shape = arrays[0].shape
+    place = lax.broadcasted_iota(jnp.int32, shape, 1) // block
+    arrays = [pltpu.roll(array, index * block, 1) if index else array for index, array in enumerate(arrays)]
+    arrays += [jnp.zeros(shape, f32)] * (count - len(arrays))
+    step = 1
+    while step < count:
+        odd = (place // step) % 2 == 1
+        arrays = [jnp.where(odd, arrays[(index + step) % count], arrays[index]) for index in range(count)]
+        step *= 2
+    return [
+        pltpu.roll(arrays[count - index], LANES - index * block, 1) if index else arrays[0] for index in range(count)
+    ]
 
 
 def exchange(arrays, block):
@@ -223,7 +268,7 @@
     for copy in copies[5:]:
         copy.wait()
     rows = []
-    for columns in transform(table_ref, win_ref[0, 1 : G + 1, :], win_ref[1, 1 : G + 1, :]):
+    for columns in transform(table_ref[...], win_ref[0, 1 : G + 1, :], win_ref[1, 1 : G + 1, :]):
         pieces = [columns[low * NX : (low + 1) * NX] for low in range(K_ONE)]
         rows += exchange(pieces, PAD_TWO)[:WIN_ONE]
     for row, piece in enumerate(pack(rows)):
@@ -237,34 +282,38 @@
 
 def second_kernel(in_ref, table_ref, out_ref):
     rows = window_rows(in_ref)
-    window = [jnp.concatenate(rows[part * WIN_ONE : (part + 1) * WIN_ONE], axis=0) for part in range(2)]
-    for part, columns in enumerate(transform(table_ref, *window)):
-        pieces = [columns[low * NY : (low + 1) * NY] for low in range(K_TWO)]
-        for cell, piece in enumerate(exchange(pieces, 1)[:WIN_TWO]):
+    parts = transform_window(table_ref, [rows[:WIN_ONE], rows[WIN_ONE:]], NX)
+    half = NY // 2
+    for part, halves in enumerate(parts):
+        pieces = [
+            jnp.concatenate([columns[low * half : (low + 1) * half] for columns in halves], axis=0)
+            for low in range(K_TWO)
+        ]
+        for cell, piece in enumerate(exchange_turned(pieces, 1, PAD_TWO)[:WIN_TWO]):
             out_ref[pl.ds(2 * cell + part, NY, stride=ROWS_Y), :] = piece
 
 
 def third_kernel(in_ref, spec_ref, table_ref, back_ref, out_ref):
-    window = [
-        jnp.concatenate([gather(in_ref, 2 * cell + part, NY, ROWS_Y) for cell in range(WIN_TWO)], axis=0)
-        for part in range(2)
+    parts = [[gather(in_ref, 2 * cell + part, NY, ROWS_Y) for cell in range(WIN_TWO)] for part in range(2)]
+    factor = spec_ref[...].reshape(LANES, LENGTH).T
+    factors = factor[:G], factor[G:]
+    scaled = [
+        [columns * factor for columns, factor in zip(halves, factors)]
+        for halves in transform_window(table_ref, parts, NY)
     ]
-    factor = spec_ref[...].reshape(LANES, LENGTH).T
-    scaled = [columns * factor for columns in transform(table_ref, *window)]
-    for part, columns in enumerate(transform(back_ref, *scaled)):
-        for cell in range(WIN_TWO):
-            out_ref[pl.ds(2 * cell + part, NY, stride=ROWS_Y), :] = columns[cell * NY : (cell + 1) * NY]
+    for part, rows in enumerate(window_transform(back_ref, scaled, WIN_TWO, NY)):
+        for cell, row in enumerate(rows):
+            out_ref[pl.ds(2 * cell + part, NY, stride=ROWS_Y), :] = row
 
 
 def fourth_kernel(in_ref, table_ref, out_ref):
     parts = []
+    half = NY // 2
     for part in range(2):
         pieces = [gather(in_ref, 2 * cell + part, NY, ROWS_Y) for cell in range(WIN_TWO)]
-        pieces += [jnp.zeros((NY, LANES), f32)] * (K_TWO - WIN_TWO)
-        parts.append(jnp.concatenate(exchange(pieces, 1), axis=0))
-    rows = []
-    for columns in transform(table_ref, *parts):
-        rows += [columns[cell * NX : (cell + 1) * NX] for cell in range(WIN_ONE)]
+        pieces = exchange_turned(pieces, 1, K_TWO)
+        parts.append([jnp.concatenate([piece[at : at + half] for piece in pieces], axis=0) for at in (0, half)])
+    rows = sum(window_transform(table_ref, parts, WIN_ONE, NX), [])
     for row, piece in enumerate(pack(rows)):
         out_ref[pl.ds(row, NX, stride=ROWS_X), :] = piece
 
@@ -280,9 +329,8 @@
     parts = []
     for part in range(2):
         pieces = rows[part * WIN_ONE : (part + 1) * WIN_ONE]
-        pieces += [jnp.zeros((NX, LANES), f32)] * (PAD_ONE - WIN_ONE)
-        parts.append(jnp.concatenate(exchange(pieces, PAD_TWO), axis=0))
-    smooth = transform(table_ref, *parts)
+        parts.append(jnp.concatenate(exchange(pieces + [jnp.zeros((NX, LANES), f32)], PAD_TWO), axis=0))
+    smooth = transform(table_ref[...], *parts)
     win_ref[...] = jnp.zeros_like(win_ref)
     for probe in range(probes):
         win_ref[probe, 1 : G + 1, :] = smooth[probe]

time: 99.7 us -> 100 us (level)
  no operation moved by 1% of the time
where the time goes in v5:
time: 100 us; the launch traced here: 99.7 us
  blocking collectives  91.4 us (91%)
  Pallas kernels  6.57 us (7%)
  local copies, waits for them, and re-layouts  1.04 us (1%)
    all_to_all x6, blocking collectives, across(): lax.all_to_all(sent, axis, split_axis=0, concat_axis=0, tiled=True)  91.4 us
    pallas_call x7, Pallas kernels, call(): pl.pallas_call(kernel, out_shape=outs, in_specs=[pl.BlockSpec(memory_spac...  6.57 us

profile of v5, /device:TPU:1, one launch (start us, length us, event | category | flops | bytes accessed | tf_op | source)
XLA Modules:
  0.0 99.7 jit_solution(13345276286625135936)
XLA Ops:
  0.6 0.0 copy-start.4
  0.6 0.0 copy-start.3
  0.7 0.0 copy-start.2
  0.7 0.0 copy-start.5
  0.7 0.0 copy-start.1
  0.7 2.7 %spread.1 = (f32[320,128]{1,0:T(8,128)S(1)}, f32[2,8,512]{2,1,0:T(8,128)S(1)}, f32[8,512]{1,0:T(8,128)S(1)}, f32[8,24,512]{2,1,0:T(8,128)S(1)}, bf16[8,256,512]{2,1,0:T(8,128)(2,1)S(1)}) custom-call(s32[1,1,8]{2,1,0:T(1,128)} %tile_far_ref.1, s32[1,1,8]{2,1,0:T(1,128)} %refs_1_.1, f32[2,1,1,8,512]{4,3,2,1,0:T(8,128)} %refs_2_.1, ...), custom_call_target="tpu_custom_call" | custom-call | flops 400000000 | bytes 8000000 | tf_op jit(solution)/shard_map/spread/pallas_call | solution.py:397
  3.4 0.0 copy-start.6
  3.4 23.1 %all_to_all.30 = f32[320,1,128]{2,1,0:T(1,128)S(1)} all-to-all(f32[320,1,128]{2,1,0:T(1,128)S(1)} %bitcast.31), channel_id=1, replica_groups=mesh['gx'=32,'gy'=16] {'gx'}, dimensions={0} | all-to-all | bytes 327680 | tf_op jit(solution)/shard_map/all_to_all | solution.py:412
  26.6 0.0 copy-start
  26.6 1.0 copy-done
  27.5 0.6 second.1
  28.1 19.3 %all_to_all.31 = f32[352,1,128]{2,1,0:T(1,128)S(1)} all-to-all(f32[352,1,128]{2,1,0:T(1,128)S(1)} %bitcast.26), channel_id=1, replica_groups=mesh['gx'=32,'gy'=16] {'gy'}, dimensions={0} | all-to-all | bytes 360448 | tf_op jit(solution)/shard_map/all_to_all | solution.py:412
  47.5 0.0 copy-done.4
  47.5 0.0 copy-done.3
  47.5 0.0 copy-done.5
  47.5 0.5 third.1
  48.0 12.7 %all_to_all.32 = f32[352,1,128]{2,1,0:T(1,128)S(1)} all-to-all(f32[352,1,128]{2,1,0:T(1,128)S(1)} %bitcast.25), channel_id=1, replica_groups=mesh['gx'=32,'gy'=16] {'gy'}, dimensions={0} | all-to-all | bytes 360448 | tf_op jit(solution)/shard_map/all_to_all | solution.py:412
  60.7 0.0 copy-done.2
  60.7 0.0 copy-start.7
  60.7 0.6 fourth.1
  61.3 13.5 %all_to_all.33 = f32[320,1,128]{2,1,0:T(1,128)S(1)} all-to-all(f32[320,1,128]{2,1,0:T(1,128)S(1)} %bitcast.29), channel_id=1, replica_groups=mesh['gx'=32,'gy'=16] {'gx'}, dimensions={0} | all-to-all | bytes 327680 | tf_op jit(solution)/shard_map/all_to_all | solution.py:412
  74.8 0.0 copy-done.1
  74.8 0.0 copy-done.6
  74.8 1.3 %read.1 = (f32[2,8,512]{2,1,0:T(8,128)S(1)}, f32[16,128]{1,0:T(8,128)S(1)}) custom-call(s32[1,1,8]{2,1,0:T(1,128)} %tile_far_ref.1, f32[320,128]{1,0:T(8,128)S(1)} %bitcast.30, f32[2,1,1,8,512]{4,3,2,1,0:T(8,128)S(1)} %copy-done.6, f32[2,8,512]{2,1,0:T(8,128)S(1)} %get-tuple-element.11.dir_ref, f32[8,512]{1,0:T(8,128)S(1)} %get-tuple-element.12.live_ref, ...), custom_call_target="tpu_custom_call" | custom-call | tf_op jit(solution)/shard_map/read/pallas_call | solution.py:397
  76.1 11.2 %all_to_all.34 = f32[16,1,128]{2,1,0:T(1,128)S(1)} all-to-all(f32[16,1,128]{2,1,0:T(1,128)S(1)} %bitcast.35), channel_id=1, replica_groups=mesh['gx'=32,'gy'=16] {'gy'}, dimensions={0} | all-to-all | bytes 16384 | tf_op jit(solution)/shard_map/all_to_all | solution.py:412
  87.3 11.6 %all_to_all.35 = f32[32,1,128]{2,1,0:T(1,128)S(1)} all-to-all(f32[32,1,128]{2,1,0:T(1,128)S(1)} %bitcast.33), channel_id=1, replica_groups=mesh['gx'=32,'gy'=16] {'gx'}, dimensions={0} | all-to-all | bytes 32768 | tf_op jit(solution)/shard_map/all_to_all | solution.py:412
  98.9 0.0 copy-done.7
  98.9 0.8 update.1
  (1 shorter events, 0.0 us)
Async XLA Ops:
  0.6 46.8 %copy-start.4 = (bf16[352,384]{1,0:T(8,128)(2,1)S(1)}, bf16[352,384]{1,0:T(8,128)(2,1)}, u32[]{:S(2)}) copy-start(bf16[352,384]{1,0:T(8,128)(2,1)} %constant.15.clone.back_ref) | copy-start | bytes 811012
  0.6 46.8 %copy-start.3 = (bf16[256,624]{1,0:T(8,128)(2,1)S(1)}, bf16[256,624]{1,0:T(8,128)(2,1)}, u32[]{:S(2)}) copy-start(bf16[256,624]{1,0:T(8,128)(2,1)} %constant.14.clone.table_ref) | copy-start | bytes 958468
  0.7 60.0 %copy-start.2 = (bf16[448,384]{1,0:T(8,128)(2,1)S(1)}, bf16[448,384]{1,0:T(8,128)(2,1)}, u32[]{:S(2)}) copy-start(bf16[448,384]{1,0:T(8,128)(2,1)} %constant.16.clone.table_ref) | copy-start | bytes 1032196
  0.7 46.8 %copy-start.5 = (f32[8,16,256]{2,1,0:T(8,128)S(1)}, f32[8,16,256]{2,1,0:T(8,128)}, u32[]{:S(2)}) copy-start(f32[8,16,256]{2,1,0:T(8,128)} %spec_ref.1) | copy-start | bytes 393220
  0.7 74.1 %copy-start.1 = (bf16[256,768]{1,0:T(8,128)(2,1)S(1)}, bf16[256,768]{1,0:T(8,128)(2,1)}, u32[]{:S(2)}) copy-start(bf16[256,768]{1,0:T(8,128)(2,1)} %constant.17.clone.table_ref) | copy-start | bytes 1179652
  3.4 71.4 %copy-start.6 = (f32[2,1,1,8,512]{4,3,2,1,0:T(8,128)S(1)}, f32[2,1,1,8,512]{4,3,2,1,0:T(8,128)}, u32[]{:S(2)}) copy-start(f32[2,1,1,8,512]{4,3,2,1,0:T(8,128)} %res_ref.3) | copy-start | bytes 98308
  26.6 1.0 copy-start
  60.7 38.2 %copy-start.7 = (f32[2,1,1,8,512]{4,3,2,1,0:T(8,128)S(1)}, f32[2,1,1,8,512]{4,3,2,1,0:T(8,128)}, u32[]{:S(2)}) copy-start(f32[2,1,1,8,512]{4,3,2,1,0:T(8,128)} %iterate_ref.1) | copy-start | bytes 98308

commit v6 on v5

--- a/solution.py
+++ b/solution.py
@@ -56,6 +56,11 @@
     return cell, (cell >= 0) & (cell < G)
 
 
+def joined(even, odd):
+    gap = np.zeros((odd.shape[0], -odd.shape[1] % LANES), ml_dtypes.bfloat16)
+    return np.concatenate([odd, gap, even], axis=1)
+
+
 def cells_of(window, parity):
     return list(range(1 - parity, window, 2))
 
@@ -69,8 +74,10 @@
     n1 = np.arange(G)
     k1_low, k1_owner = grid(K_ONE, NX)
     k1 = k1_owner * K_ONE + k1_low
-    first = table(k1, yes(k1), n1, yes(n1), -1.0, 1.0)
     first_back = table(n1, yes(n1), k1, yes(k1), 1.0, 1.0 / LENGTH)
+    k1_low, k1_owner = grid(K_ONE, NX // 2)
+    k1 = k1_owner * K_ONE + k1_low
+    first = joined(*[table(k1, yes(k1), n, yes(n), -1.0, 1.0) for n in (n1[0::2], n1[1::2])])
     k2_low, k2_owner = grid(K_TWO, NY // 2)
     k2 = k2_owner * K_TWO + k2_low
     k3 = np.arange(LENGTH // 2)
@@ -82,8 +89,7 @@
             n, n_ok = window_index(owner, 2 * cell + 1 - parity, wide)
             out.append(table(k, yes(k), n, n_ok, -1.0, 1.0))
             back.append(table(n, n_ok, k, yes(k), 1.0, 1.0 / LENGTH))
-        gap = np.zeros((out[1].shape[0], -out[1].shape[1] % LANES), ml_dtypes.bfloat16)
-        wholes.append((np.concatenate([out[1], gap, out[0]], axis=1), np.concatenate(back, axis=0)))
+        wholes.append((joined(*out), np.concatenate(back, axis=0)))
     return first, wholes[0][0], wholes[1][0], wholes[1][1], wholes[0][1], first_back
 
 
@@ -104,15 +110,30 @@
     return cos[:, :LANES] - sin[:, LANES:], cos[:, LANES:] + sin[:, :LANES]
 
 
-def transform_window(table_ref, parts, owners):
+def transform_cells(table_ref, cells):
     results = []
-    for parity in range(2):
-        places = cells_of(len(parts[0]), parity)
-        depth = 3 * len(places) * owners
+    for parity, parts in enumerate(cells):
+        depth = 3 * parts[0].shape[0]
         start = 0 if parity else table_ref.shape[1] - depth
-        data = [jnp.concatenate([rows[place] for place in places], axis=0) for rows in parts]
-        results.append(transform(table_ref[:, start : start + depth], *data))
+        results.append(transform(table_ref[:, start : start + depth], *parts))
     return [(even + odd, even - odd) for even, odd in zip(*results)]
+
+
+def transform_window(table_ref, parts):
+    return transform_cells(
+        table_ref,
+        [
+            [jnp.concatenate([rows[place] for place in cells_of(len(rows), parity)], axis=0) for rows in parts]
+            for parity in range(2)
+        ],
+    )
+
+
+def by_owner(halves, owners, count):
+    half = owners // 2
+    return [
+        jnp.concatenate([columns[low * half : (low + 1) * half] for columns in halves], axis=0) for low in range(count)
+    ]
 
 
 def window_transform(table_ref, parts, window, owners):
@@ -267,9 +288,10 @@
             win_ref[probe, place, :] += total[probe * SPAN : (probe + 1) * SPAN]
     for copy in copies[5:]:
         copy.wait()
+    cells = [[win_ref[probe, pl.ds(1 + parity, G // 2, stride=2), :] for probe in range(probes)] for parity in range(2)]
     rows = []
-    for columns in transform(table_ref[...], win_ref[0, 1 : G + 1, :], win_ref[1, 1 : G + 1, :]):
-        pieces = [columns[low * NX : (low + 1) * NX] for low in range(K_ONE)]
+    for halves in transform_cells(table_ref, cells):
+        pieces = by_owner(halves, NX, K_ONE)
         rows += exchange(pieces, PAD_TWO)[:WIN_ONE]
     for row, piece in enumerate(pack(rows)):
         out_ref[pl.ds(row, NX, stride=ROWS_X), :] = piece
@@ -282,13 +304,9 @@
 
 def second_kernel(in_ref, table_ref, out_ref):
     rows = window_rows(in_ref)
-    parts = transform_window(table_ref, [rows[:WIN_ONE], rows[WIN_ONE:]], NX)
-    half = NY // 2
+    parts = transform_window(table_ref, [rows[:WIN_ONE], rows[WIN_ONE:]])
     for part, halves in enumerate(parts):
-        pieces = [
-            jnp.concatenate([columns[low * half : (low + 1) * half] for columns in halves], axis=0)
-            for low in range(K_TWO)
-        ]
+        pieces = by_owner(halves, NY, K_TWO)
         for cell, piece in enumerate(exchange_turned(pieces, 1, PAD_TWO)[:WIN_TWO]):
             out_ref[pl.ds(2 * cell + part, NY, stride=ROWS_Y), :] = piece
 
@@ -299,7 +317,7 @@
     factors = factor[:G], factor[G:]
     scaled = [
         [columns * factor for columns, factor in zip(halves, factors)]
-        for halves in transform_window(table_ref, parts, NY)
+        for halves in transform_window(table_ref, parts)
     ]
     for part, rows in enumerate(window_transform(back_ref, scaled, WIN_TWO, NY)):
         for cell, row in enumerate(rows):
@@ -432,7 +450,7 @@
         ],
         operands,
         far=len(operands),
-        cost=pl.CostEstimate(flops=400_000_000, bytes_accessed=8_000_000, transcendentals=0),
+        cost=pl.CostEstimate(flops=4_000_000_000, bytes_accessed=24_000_000, transcendentals=0),
         scratch=(*near, window, pltpu.SemaphoreType.DMA((len(operands),))),
     )
     came = across("gx", sent)

time: 100 us -> 99.1 us (level)
  no operation moved by 1% of the time
where the time goes in v6:
time: 99.1 us; the launch traced here: 98.8 us
  blocking collectives  91.5 us (92%)
  Pallas kernels  6.52 us (7%)
    all_to_all x6, blocking collectives, across(): lax.all_to_all(sent, axis, split_axis=0, concat_axis=0, tiled=True)  91.5 us
    pallas_call x7, Pallas kernels, call(): pl.pallas_call(kernel, out_shape=outs, in_specs=[pl.BlockSpec(memory_spac...  6.52 us

profile of v6, /device:TPU:1, one launch (start us, length us, event | category | flops | bytes accessed | tf_op | source)
XLA Modules:
  0.0 98.8 jit_solution(1254186212576108549)
XLA Ops:
  0.6 0.0 copy-start
  0.6 0.0 copy-start.3
  0.7 0.0 copy-start.4
  0.7 0.0 copy-start.5
  0.7 2.7 %spread.1 = (f32[320,128]{1,0:T(8,128)S(1)}, f32[2,8,512]{2,1,0:T(8,128)S(1)}, f32[8,512]{1,0:T(8,128)S(1)}, f32[8,24,512]{2,1,0:T(8,128)S(1)}, bf16[8,256,512]{2,1,0:T(8,128)(2,1)S(1)}) custom-call(s32[1,1,8]{2,1,0:T(1,128)} %tile_far_ref.1, s32[1,1,8]{2,1,0:T(1,128)} %refs_1_.1, f32[2,1,1,8,512]{4,3,2,1,0:T(8,128)} %refs_2_.1, ...), custom_call_target="tpu_custom_call" | custom-call | flops 4000000000 | bytes 24000000 | tf_op jit(solution)/shard_map/spread/pallas_call | solution.py:415
  3.3 0.0 copy-start.2
  3.4 0.0 copy-start.1
  3.4 0.0 copy-start.6
  3.4 23.2 %all_to_all.30 = f32[320,1,128]{2,1,0:T(1,128)S(1)} all-to-all(f32[320,1,128]{2,1,0:T(1,128)S(1)} %bitcast.31), channel_id=1, replica_groups=mesh['gx'=32,'gy'=16] {'gx'}, dimensions={0} | all-to-all | bytes 327680 | tf_op jit(solution)/shard_map/all_to_all | solution.py:430
  26.6 0.0 copy-done
  26.6 0.6 second.1
  27.2 19.3 %all_to_all.31 = f32[352,1,128]{2,1,0:T(1,128)S(1)} all-to-all(f32[352,1,128]{2,1,0:T(1,128)S(1)} %bitcast.26), channel_id=1, replica_groups=mesh['gx'=32,'gy'=16] {'gy'}, dimensions={0} | all-to-all | bytes 360448 | tf_op jit(solution)/shard_map/all_to_all | solution.py:430
  46.6 0.0 copy-done.3
  46.6 0.0 copy-done.4
  46.6 0.0 copy-done.5
  46.6 0.5 third.1
  47.1 12.6 %all_to_all.32 = f32[352,1,128]{2,1,0:T(1,128)S(1)} all-to-all(f32[352,1,128]{2,1,0:T(1,128)S(1)} %bitcast.25), channel_id=1, replica_groups=mesh['gx'=32,'gy'=16] {'gy'}, dimensions={0} | all-to-all | bytes 360448 | tf_op jit(solution)/shard_map/all_to_all | solution.py:430
  59.8 0.0 copy-done.2
  59.8 0.0 copy-start.7
  59.8 0.6 fourth.1
  60.4 13.5 %all_to_all.33 = f32[320,1,128]{2,1,0:T(1,128)S(1)} all-to-all(f32[320,1,128]{2,1,0:T(1,128)S(1)} %bitcast.29), channel_id=1, replica_groups=mesh['gx'=32,'gy'=16] {'gx'}, dimensions={0} | all-to-all | bytes 327680 | tf_op jit(solution)/shard_map/all_to_all | solution.py:430
  73.8 0.0 copy-done.1
  73.8 0.0 copy-done.6
  73.8 1.3 %read.1 = (f32[2,8,512]{2,1,0:T(8,128)S(1)}, f32[16,128]{1,0:T(8,128)S(1)}) custom-call(s32[1,1,8]{2,1,0:T(1,128)} %tile_far_ref.1, f32[320,128]{1,0:T(8,128)S(1)} %bitcast.30, f32[2,1,1,8,512]{4,3,2,1,0:T(8,128)S(1)} %copy-done.6, f32[2,8,512]{2,1,0:T(8,128)S(1)} %get-tuple-element.11.dir_ref, f32[8,512]{1,0:T(8,128)S(1)} %get-tuple-element.12.live_ref, ...), custom_call_target="tpu_custom_call" | custom-call | tf_op jit(solution)/shard_map/read/pallas_call | solution.py:415
  75.1 11.2 %all_to_all.34 = f32[16,1,128]{2,1,0:T(1,128)S(1)} all-to-all(f32[16,1,128]{2,1,0:T(1,128)S(1)} %bitcast.35), channel_id=1, replica_groups=mesh['gx'=32,'gy'=16] {'gy'}, dimensions={0} | all-to-all | bytes 16384 | tf_op jit(solution)/shard_map/all_to_all | solution.py:430
  86.3 11.6 %all_to_all.35 = f32[32,1,128]{2,1,0:T(1,128)S(1)} all-to-all(f32[32,1,128]{2,1,0:T(1,128)S(1)} %bitcast.33), channel_id=1, replica_groups=mesh['gx'=32,'gy'=16] {'gx'}, dimensions={0} | all-to-all | bytes 32768 | tf_op jit(solution)/shard_map/all_to_all | solution.py:430
  97.9 0.0 copy-done.7
  97.9 0.8 update.1
  (1 shorter events, 0.0 us)
Async XLA Ops:
  0.6 26.0 %copy-start = (bf16[256,672]{1,0:T(8,128)(2,1)S(1)}, bf16[256,672]{1,0:T(8,128)(2,1)}, u32[]{:S(2)}) copy-start(bf16[256,672]{1,0:T(8,128)(2,1)} %constant.13.clone.table_ref) | copy-start | bytes 1032196
  0.6 45.9 %copy-start.3 = (bf16[256,624]{1,0:T(8,128)(2,1)S(1)}, bf16[256,624]{1,0:T(8,128)(2,1)}, u32[]{:S(2)}) copy-start(bf16[256,624]{1,0:T(8,128)(2,1)} %constant.14.clone.table_ref) | copy-start | bytes 958468
  0.7 45.9 %copy-start.4 = (bf16[352,384]{1,0:T(8,128)(2,1)S(1)}, bf16[352,384]{1,0:T(8,128)(2,1)}, u32[]{:S(2)}) copy-start(bf16[352,384]{1,0:T(8,128)(2,1)} %constant.15.clone.back_ref) | copy-start | bytes 811012
  0.7 45.9 %copy-start.5 = (f32[8,16,256]{2,1,0:T(8,128)S(1)}, f32[8,16,256]{2,1,0:T(8,128)}, u32[]{:S(2)}) copy-start(f32[8,16,256]{2,1,0:T(8,128)} %spec_ref.1) | copy-start | bytes 393220
  3.3 56.4 %copy-start.2 = (bf16[448,384]{1,0:T(8,128)(2,1)S(1)}, bf16[448,384]{1,0:T(8,128)(2,1)}, u32[]{:S(2)}) copy-start(bf16[448,384]{1,0:T(8,128)(2,1)} %constant.16.clone.table_ref) | copy-start | bytes 1032196
  3.4 70.5 %copy-start.1 = (bf16[256,768]{1,0:T(8,128)(2,1)S(1)}, bf16[256,768]{1,0:T(8,128)(2,1)}, u32[]{:S(2)}) copy-start(bf16[256,768]{1,0:T(8,128)(2,1)} %constant.17.clone.table_ref) | copy-start | bytes 1179652
  3.4 70.5 %copy-start.6 = (f32[2,1,1,8,512]{4,3,2,1,0:T(8,128)S(1)}, f32[2,1,1,8,512]{4,3,2,1,0:T(8,128)}, u32[]{:S(2)}) copy-start(f32[2,1,1,8,512]{4,3,2,1,0:T(8,128)} %res_ref.3) | copy-start | bytes 98308
  59.8 38.2 %copy-start.7 = (f32[2,1,1,8,512]{4,3,2,1,0:T(8,128)S(1)}, f32[2,1,1,8,512]{4,3,2,1,0:T(8,128)}, u32[]{:S(2)}) copy-start(f32[2,1,1,8,512]{4,3,2,1,0:T(8,128)} %iterate_ref.1) | copy-start | bytes 98308

commit v7 on v6

--- a/solution.py
+++ b/solution.py
@@ -260,9 +260,10 @@
 
 def spread_kernel(*refs):
     outside, refs = refs[:6], refs[6:]
-    out_ref, masked_ref, live_ref, depth_ref, plane_ref, *inside, win_ref, sems = refs
+    out_ref, masked_ref, live_ref, depth_ref, plane_ref, near_tile_ref, *inside, win_ref, sems = refs
     tile_ref, count_ref, dir_ref, cells_ref, fracs_ref, table_ref = inside
     copies = [pltpu.make_async_copy(far, near, sems.at[at]) for at, (far, near) in enumerate(zip(outside, inside))]
+    copies.append(pltpu.make_async_copy(outside[0], near_tile_ref, sems.at[len(copies)]))
     for copy in copies:
         copy.start()
     win_ref[...] = jnp.zeros_like(win_ref)
@@ -337,24 +338,24 @@
 
 
 def read_kernel(
-    tile_far_ref, in_ref, res_ref, dir_ref, live_ref, depth_ref, plane_ref, table_ref,
-    image_ref, sums_ref, tile_ref, win_ref, sems,
+    near_tile_ref, in_ref, res_ref, dir_ref, live_ref, depth_ref, plane_ref, table_ref,
+    image_ref, sums_ref, win_ref,
 ):
-    copy = pltpu.make_async_copy(tile_far_ref, tile_ref, sems.at[0])
-    copy.start()
+    tile_row = near_tile_ref[0]
+    own = lax.broadcasted_iota(jnp.int32, tile_row.shape, 1)
+    tiles = [jnp.max(jnp.where(own == slot, tile_row, 0)) for slot in range(tile_row.shape[1])]
     probes, slots = image_ref.shape[:2]
     rows = window_rows(in_ref)
     parts = []
     for part in range(2):
         pieces = rows[part * WIN_ONE : (part + 1) * WIN_ONE]
-        parts.append(jnp.concatenate(exchange(pieces + [jnp.zeros((NX, LANES), f32)], PAD_TWO), axis=0))
+        parts.append(jnp.concatenate(exchange_turned(pieces, PAD_TWO, K_ONE), axis=0))
     smooth = transform(table_ref[...], *parts)
     win_ref[...] = jnp.zeros_like(win_ref)
     for probe in range(probes):
         win_ref[probe, 1 : G + 1, :] = smooth[probe]
-    copy.wait()
     for slot in range(slots):
-        place = pl.ds(pl.multiple_of(tile_ref[0, 0, slot] * TL, TL), SPAN)
+        place = pl.ds(pl.multiple_of(tiles[slot] * TL, TL), SPAN)
         block = jnp.concatenate([win_ref[probe, place, :] for probe in range(probes)], axis=0)
         block_high, block_low = split(block)
         rows = block.shape[0]
@@ -438,7 +439,7 @@
     near = [
         (pltpu.SMEM if at < 2 else pltpu.VMEM)(operand.shape, operand.dtype) for at, operand in enumerate(operands)
     ]
-    sent, masked, live, depth, planes = call(
+    sent, masked, live, depth, planes, near_tile = call(
         spread_kernel,
         "spread",
         [
@@ -447,11 +448,12 @@
             (slots, cap),
             (slots, SPAN, cap),
             ((slots, 2 * LANES, cap), bf16),
+            (slot_tile.shape, slot_tile.dtype),
         ],
         operands,
         far=len(operands),
         cost=pl.CostEstimate(flops=4_000_000_000, bytes_accessed=24_000_000, transcendentals=0),
-        scratch=(*near, window, pltpu.SemaphoreType.DMA((len(operands),))),
+        scratch=(*near, window, pltpu.SemaphoreType.DMA((len(operands) + 1,))),
     )
     came = across("gx", sent)
     (sent,) = call(second_kernel, "second", [(NY * ROWS_Y, LANES)], (came, second))
@@ -464,9 +466,8 @@
         read_kernel,
         "read",
         [(probes, slots, cap), (NY, LANES)],
-        (slot_tile, came, residual, masked, live, depth, planes, first_back),
-        far=1,
-        scratch=(near[0], window, pltpu.SemaphoreType.DMA((1,))),
+        (near_tile, came, residual, masked, live, depth, planes, first_back),
+        scratch=(window,),
     )
     sums = across("gy", sums)
     (sums,) = call(total_kernel, "total", [(NX, LANES)], (sums,))

time: 99.1 us -> 99 us (level)
  no operation moved by 1% of the time
where the time goes in v7:
time: 99 us; the launch traced here: 98.6 us
  blocking collectives  91.5 us (92%)
  Pallas kernels  6.4 us (6%)
    all_to_all x6, blocking collectives, across(): lax.all_to_all(sent, axis, split_axis=0, concat_axis=0, tiled=True)  91.5 us
    pallas_call x7, Pallas kernels, call(): pl.pallas_call(kernel, out_shape=outs, in_specs=[pl.BlockSpec(memory_spac...  6.4 us

profile of v7, /device:TPU:1, one launch (start us, length us, event | category | flops | bytes accessed | tf_op | source)
XLA Modules:
  0.0 98.6 jit_solution(11502241571008620717)
XLA Ops:
  0.6 0.0 copy-start
  0.6 0.0 copy-start.3
  0.7 0.0 copy-start.4
  0.7 0.0 copy-start.5
  0.7 2.7 %spread.1 = (f32[320,128]{1,0:T(8,128)S(1)}, f32[2,8,512]{2,1,0:T(8,128)S(1)}, f32[8,512]{1,0:T(8,128)S(1)}, f32[8,24,512]{2,1,0:T(8,128)S(1)}, bf16[8,256,512]{...) custom-call(s32[1,1,8]{2,1,0:T(1,128)} %refs_0_.1, s32[1,1,8]{2,1,0:T(1,128)} %refs_1_.1, f32[2,1,1,8,512]{4,3,2,1,0:T(8,128)} %refs_2_.1, ...), custom_call_target="tpu_custom_call" | custom-call | flops 4000000000 | bytes 24000000 | tf_op jit(solution)/shard_map/spread/pallas_call | solution.py:416
  3.4 0.0 copy-start.2
  3.4 0.0 copy-start.1
  3.4 0.0 copy-start.6
  3.4 23.3 %all_to_all.30 = f32[320,1,128]{2,1,0:T(1,128)S(1)} all-to-all(f32[320,1,128]{2,1,0:T(1,128)S(1)} %bitcast.31), channel_id=1, replica_groups=mesh['gx'=32,'gy'=16] {'gx'}, dimensions={0} | all-to-all | bytes 327680 | tf_op jit(solution)/shard_map/all_to_all | solution.py:431
  26.7 0.0 copy-done
  26.7 0.6 second.1
  27.3 19.3 %all_to_all.31 = f32[352,1,128]{2,1,0:T(1,128)S(1)} all-to-all(f32[352,1,128]{2,1,0:T(1,128)S(1)} %bitcast.26), channel_id=1, replica_groups=mesh['gx'=32,'gy'=16] {'gy'}, dimensions={0} | all-to-all | bytes 360448 | tf_op jit(solution)/shard_map/all_to_all | solution.py:431
  46.6 0.0 copy-done.3
  46.6 0.0 copy-done.4
  46.6 0.0 copy-done.5
  46.6 0.5 third.1
  47.1 12.6 %all_to_all.32 = f32[352,1,128]{2,1,0:T(1,128)S(1)} all-to-all(f32[352,1,128]{2,1,0:T(1,128)S(1)} %bitcast.25), channel_id=1, replica_groups=mesh['gx'=32,'gy'=16] {'gy'}, dimensions={0} | all-to-all | bytes 360448 | tf_op jit(solution)/shard_map/all_to_all | solution.py:431
  59.8 0.0 copy-done.2
  59.8 0.0 copy-start.7
  59.8 0.6 fourth.1
  60.4 13.5 %all_to_all.33 = f32[320,1,128]{2,1,0:T(1,128)S(1)} all-to-all(f32[320,1,128]{2,1,0:T(1,128)S(1)} %bitcast.29), channel_id=1, replica_groups=mesh['gx'=32,'gy'=16] {'gx'}, dimensions={0} | all-to-all | bytes 327680 | tf_op jit(solution)/shard_map/all_to_all | solution.py:431
  73.9 0.0 copy-done.1
  73.9 0.0 copy-done.6
  73.9 1.2 %read.1 = (f32[2,8,512]{2,1,0:T(8,128)S(1)}, f32[16,128]{1,0:T(8,128)S(1)}) custom-call(s32[1,1,8]{2,1,0:T(1,128)S(1)} %get-tuple-element.11.near_tile_ref, f32[320,128]{1,0:T(8,128)S(1)} %bitcast.30, f32[2,1,1,8,512]{4,3,2,1,0:T(8,128)S(1)} %copy-done.6, f32[2,8,512]{2,1,0:T(8,128)S(1)} %get-tuple-element.13.dir_ref, ...), custom_call_target="tpu_custom_call" | custom-call | tf_op jit(solution)/shard_map/read/pallas_call | solution.py:416
  75.0 11.2 %all_to_all.34 = f32[16,1,128]{2,1,0:T(1,128)S(1)} all-to-all(f32[16,1,128]{2,1,0:T(1,128)S(1)} %bitcast.35), channel_id=1, replica_groups=mesh['gx'=32,'gy'=16] {'gy'}, dimensions={0} | all-to-all | bytes 16384 | tf_op jit(solution)/shard_map/all_to_all | solution.py:431
  86.2 11.6 %all_to_all.35 = f32[32,1,128]{2,1,0:T(1,128)S(1)} all-to-all(f32[32,1,128]{2,1,0:T(1,128)S(1)} %bitcast.33), channel_id=1, replica_groups=mesh['gx'=32,'gy'=16] {'gx'}, dimensions={0} | all-to-all | bytes 32768 | tf_op jit(solution)/shard_map/all_to_all | solution.py:431
  97.8 0.0 copy-done.7
  97.8 0.8 update.1
  (1 shorter events, 0.0 us)
Async XLA Ops:
  0.6 26.0 %copy-start = (bf16[256,672]{1,0:T(8,128)(2,1)S(1)}, bf16[256,672]{1,0:T(8,128)(2,1)}, u32[]{:S(2)}) copy-start(bf16[256,672]{1,0:T(8,128)(2,1)} %constant.13.clone.table_ref) | copy-start | bytes 1032196
  0.6 45.9 %copy-start.3 = (bf16[256,624]{1,0:T(8,128)(2,1)S(1)}, bf16[256,624]{1,0:T(8,128)(2,1)}, u32[]{:S(2)}) copy-start(bf16[256,624]{1,0:T(8,128)(2,1)} %constant.14.clone.table_ref) | copy-start | bytes 958468
  0.7 45.9 %copy-start.4 = (bf16[352,384]{1,0:T(8,128)(2,1)S(1)}, bf16[352,384]{1,0:T(8,128)(2,1)}, u32[]{:S(2)}) copy-start(bf16[352,384]{1,0:T(8,128)(2,1)} %constant.15.clone.back_ref) | copy-start | bytes 811012
  0.7 45.9 %copy-start.5 = (f32[8,16,256]{2,1,0:T(8,128)S(1)}, f32[8,16,256]{2,1,0:T(8,128)}, u32[]{:S(2)}) copy-start(f32[8,16,256]{2,1,0:T(8,128)} %spec_ref.1) | copy-start | bytes 393220
  3.4 56.4 %copy-start.2 = (bf16[448,384]{1,0:T(8,128)(2,1)S(1)}, bf16[448,384]{1,0:T(8,128)(2,1)}, u32[]{:S(2)}) copy-start(bf16[448,384]{1,0:T(8,128)(2,1)} %constant.16.clone.table_ref) | copy-start | bytes 1032196
  3.4 70.5 %copy-start.1 = (bf16[256,768]{1,0:T(8,128)(2,1)S(1)}, bf16[256,768]{1,0:T(8,128)(2,1)}, u32[]{:S(2)}) copy-start(bf16[256,768]{1,0:T(8,128)(2,1)} %constant.17.clone.table_ref) | copy-start | bytes 1179652
  3.4 70.5 %copy-start.6 = (f32[2,1,1,8,512]{4,3,2,1,0:T(8,128)S(1)}, f32[2,1,1,8,512]{4,3,2,1,0:T(8,128)}, u32[]{:S(2)}) copy-start(f32[2,1,1,8,512]{4,3,2,1,0:T(8,128)} %res_ref.3) | copy-start | bytes 98308
  59.8 38.0 %copy-start.7 = (f32[2,1,1,8,512]{4,3,2,1,0:T(8,128)S(1)}, f32[2,1,1,8,512]{4,3,2,1,0:T(8,128)}, u32[]{:S(2)}) copy-start(f32[2,1,1,8,512]{4,3,2,1,0:T(8,128)} %iterate_ref.1) | copy-start | bytes 98308

commit v8 on v7

--- a/solution.py
+++ b/solution.py
@@ -388,10 +388,6 @@
     sums_ref[...] = jnp.broadcast_to(row, sums_ref.shape)
 
 
-def total_kernel(in_ref, out_ref):
-    out_ref[...] = jnp.broadcast_to(jnp.sum(in_ref[...], axis=0, keepdims=True), out_ref.shape)
-
-
 def update_kernel(
     sums_ref, image_ref, live_ref, iterate_ref, res_ref, dir_ref, new_iterate_ref, new_res_ref, new_dir_ref
 ):
@@ -465,13 +461,11 @@
     image, sums = call(
         read_kernel,
         "read",
-        [(probes, slots, cap), (NY, LANES)],
+        [(probes, slots, cap), (NX * NY, LANES)],
         (near_tile, came, residual, masked, live, depth, planes, first_back),
         scratch=(window,),
     )
-    sums = across("gy", sums)
-    (sums,) = call(total_kernel, "total", [(NX, LANES)], (sums,))
-    sums = across("gx", sums)
+    sums = across(("gx", "gy"), sums)
     return tuple(call(update_kernel, "update", [direction.shape] * 3, (sums, image, live, iterate, residual, masked)))
 
 

time: 99 us -> 104 us (1.051)
  blocking collectives: 91.5 us -> 96.5 us
    all_to_all x6 -> x5, blocking collectives: 91.5 us -> 96.5 us  [across(): lax.all_to_all(sent, axis, split_axis=0, concat_axis=0, tiled=True)]
    pallas_call x7 -> x6, Pallas kernels: 6.4 us -> 6.46 us  [call(): pl.pallas_call(kernel, out_shape=outs, in_specs=[pl.BlockSpec(memory_spac...]
where the time goes in v8:
time: 104 us
  blocking collectives  96.5 us (93%)
  Pallas kernels  6.46 us (6%)
    all_to_all x5, blocking collectives, across(): lax.all_to_all(sent, axis, split_axis=0, concat_axis=0, tiled=True)  96.5 us
    pallas_call x6, Pallas kernels, call(): pl.pallas_call(kernel, out_shape=outs, in_specs=[pl.BlockSpec(memory_spac...  6.46 us

profile of v8, /device:TPU:1, one launch (start us, length us, event | category | flops | bytes accessed | tf_op | source)
XLA Modules:
  0.0 103.7 jit_solution(14270920502633577862)
XLA Ops:
  0.6 0.0 copy-start
  0.6 0.0 copy-start.3
  0.7 0.0 copy-start.4
  0.7 0.0 copy-start.5
  0.7 2.7 %spread.1 = (f32[320,128]{1,0:T(8,128)S(1)}, f32[2,8,512]{2,1,0:T(8,128)S(1)}, f32[8,512]{1,0:T(8,128)S(1)}, f32[8,24,512]{2,1,0:T(8,128)S(1)}, bf16[8,256,512]{...) custom-call(s32[1,1,8]{2,1,0:T(1,128)} %refs_0_.1, s32[1,1,8]{2,1,0:T(1,128)} %refs_1_.1, f32[2,1,1,8,512]{4,3,2,1,0:T(8,128)} %refs_2_.1, ...), custom_call_target="tpu_custom_call" | custom-call | flops 4000000000 | bytes 24000000 | tf_op jit(solution)/shard_map/spread/pallas_call | solution.py:412
  3.4 0.0 copy-start.2
  3.4 0.0 copy-start.1
  3.4 0.0 copy-start.6
  3.4 23.3 %all_to_all.25 = f32[320,1,128]{2,1,0:T(1,128)S(1)} all-to-all(f32[320,1,128]{2,1,0:T(1,128)S(1)} %bitcast.29), channel_id=1, replica_groups=mesh['gx'=32,'gy'=16] {'gx'}, dimensions={0} | all-to-all | bytes 327680 | tf_op jit(solution)/shard_map/all_to_all | solution.py:427
  26.6 0.0 copy-done
  26.6 0.6 second.1
  27.2 19.3 %all_to_all.26 = f32[352,1,128]{2,1,0:T(1,128)S(1)} all-to-all(f32[352,1,128]{2,1,0:T(1,128)S(1)} %bitcast.23), channel_id=1, replica_groups=mesh['gx'=32,'gy'=16] {'gy'}, dimensions={0} | all-to-all | bytes 360448 | tf_op jit(solution)/shard_map/all_to_all | solution.py:427
  46.6 0.0 copy-done.3
  46.6 0.0 copy-done.4
  46.6 0.0 copy-done.5
  46.6 0.5 third.1
  47.1 12.6 %all_to_all.27 = f32[352,1,128]{2,1,0:T(1,128)S(1)} all-to-all(f32[352,1,128]{2,1,0:T(1,128)S(1)} %bitcast.22), channel_id=1, replica_groups=mesh['gx'=32,'gy'=16] {'gy'}, dimensions={0} | all-to-all | bytes 360448 | tf_op jit(solution)/shard_map/all_to_all | solution.py:427
  59.8 0.0 copy-done.2
  59.8 0.6 fourth.1
  60.4 0.0 copy-start.7
  60.4 13.5 %all_to_all.28 = f32[320,1,128]{2,1,0:T(1,128)S(1)} all-to-all(f32[320,1,128]{2,1,0:T(1,128)S(1)} %bitcast.26), channel_id=1, replica_groups=mesh['gx'=32,'gy'=16] {'gx'}, dimensions={0} | all-to-all | bytes 327680 | tf_op jit(solution)/shard_map/all_to_all | solution.py:427
  73.9 0.0 copy-done.1
  73.9 0.0 copy-done.6
  73.9 1.2 %read.1 = (f32[2,8,512]{2,1,0:T(8,128)S(1)}, f32[512,128]{1,0:T(8,128)S(1)}) custom-call(s32[1,1,8]{2,1,0:T(1,128)S(1)} %get-tuple-element.11.near_tile_ref, f32[320,128]{1,0:T(8,128)S(1)} %bitcast.27, f32[2,1,1,8,512]{4,3,2,1,0:T(8,128)S(1)} %copy-done.6, f32[2,8,512]{2,1,0:T(8,128)S(1)} %get-tuple-element.13.dir_ref, ...), custom_call_target="tpu_custom_call" | custom-call | tf_op jit(solution)/shard_map/read/pallas_call | solution.py:412
  75.1 27.8 %all_to_all.29 = f32[512,1,128]{2,1,0:T(1,128)S(1)} all-to-all(f32[512,1,128]{2,1,0:T(1,128)S(1)} %bitcast.28), channel_id=1, replica_groups=mesh['gx'=32,'gy'=16] {'gx','gy'}, dimensions={0} | all-to-all | bytes 524288 | tf_op jit(solution)/shard_map/all_to_all | solution.py:427
  102.9 0.0 copy-done.7
  102.9 0.9 update.1
Async XLA Ops:
  0.6 26.0 %copy-start = (bf16[256,672]{1,0:T(8,128)(2,1)S(1)}, bf16[256,672]{1,0:T(8,128)(2,1)}, u32[]{:S(2)}) copy-start(bf16[256,672]{1,0:T(8,128)(2,1)} %constant.13.clone.table_ref) | copy-start | bytes 1032196
  0.6 45.9 %copy-start.3 = (bf16[256,624]{1,0:T(8,128)(2,1)S(1)}, bf16[256,624]{1,0:T(8,128)(2,1)}, u32[]{:S(2)}) copy-start(bf16[256,624]{1,0:T(8,128)(2,1)} %constant.14.clone.table_ref) | copy-start | bytes 958468
  0.7 45.9 %copy-start.4 = (bf16[352,384]{1,0:T(8,128)(2,1)S(1)}, bf16[352,384]{1,0:T(8,128)(2,1)}, u32[]{:S(2)}) copy-start(bf16[352,384]{1,0:T(8,128)(2,1)} %constant.15.clone.back_ref) | copy-start | bytes 811012
  0.7 45.9 %copy-start.5 = (f32[8,16,256]{2,1,0:T(8,128)S(1)}, f32[8,16,256]{2,1,0:T(8,128)}, u32[]{:S(2)}) copy-start(f32[8,16,256]{2,1,0:T(8,128)} %spec_ref.1) | copy-start | bytes 393220
  3.4 56.4 %copy-start.2 = (bf16[448,384]{1,0:T(8,128)(2,1)S(1)}, bf16[448,384]{1,0:T(8,128)(2,1)}, u32[]{:S(2)}) copy-start(bf16[448,384]{1,0:T(8,128)(2,1)} %constant.16.clone.table_ref) | copy-start | bytes 1032196
  3.4 70.5 %copy-start.1 = (bf16[256,768]{1,0:T(8,128)(2,1)S(1)}, bf16[256,768]{1,0:T(8,128)(2,1)}, u32[]{:S(2)}) copy-start(bf16[256,768]{1,0:T(8,128)(2,1)} %constant.17.clone.table_ref) | copy-start | bytes 1179652
  3.4 70.5 %copy-start.6 = (f32[2,1,1,8,512]{4,3,2,1,0:T(8,128)S(1)}, f32[2,1,1,8,512]{4,3,2,1,0:T(8,128)}, u32[]{:S(2)}) copy-start(f32[2,1,1,8,512]{4,3,2,1,0:T(8,128)} %res_ref.3) | copy-start | bytes 98308
  60.4 42.5 %copy-start.7 = (f32[2,1,1,8,512]{4,3,2,1,0:T(8,128)S(1)}, f32[2,1,1,8,512]{4,3,2,1,0:T(8,128)}, u32[]{:S(2)}) copy-start(f32[2,1,1,8,512]{4,3,2,1,0:T(8,128)} %iterate_ref.1) | copy-start | bytes 98308

commit v9 on v7

--- a/solution.py
+++ b/solution.py
@@ -252,8 +252,8 @@
         depth = stencil(firsts[0], taps[0], slot, SPAN)
         across = stencil(firsts[1], taps[1], slot, PAD_ONE)
         upward = stencil(firsts[2], taps[2], slot, PAD_TWO)
-        plane = across[:, None, :] * upward[None, :, :]
-        return depth, plane.reshape(LANES, plane.shape[2])
+        plane = across[:WIN_ONE, None, :] * upward[None, :, :]
+        return depth, plane.reshape(WIN_ONE * PAD_TWO, plane.shape[2])
 
     return weights
 
@@ -278,7 +278,9 @@
     weights = point_weights(cells_ref, fracs_ref)
     for slot in range(slots):
         depth, plane = weights(slot)
-        planes = jnp.concatenate(split(plane), axis=0)
+        high, low = split(plane)
+        rest = jnp.zeros((LANES - plane.shape[0], plane.shape[1]), bf16)
+        planes = jnp.concatenate([high, rest, low, rest], axis=0)
         depth_ref[slot], plane_ref[slot] = depth, planes
         values = jnp.concatenate([depth * masked[probe][slot : slot + 1] for probe in range(probes)], axis=0)
         rows = values.shape[0]

time: 99 us -> 98.9 us (level)
  no operation moved by 1% of the time
where the time goes in v9:
time: 98.9 us; the launch traced here: 98.6 us
  blocking collectives  91.5 us (93%)
  Pallas kernels  6.34 us (6%)
    all_to_all x6, blocking collectives, across(): lax.all_to_all(sent, axis, split_axis=0, concat_axis=0, tiled=True)  91.5 us
    pallas_call x7, Pallas kernels, call(): pl.pallas_call(kernel, out_shape=outs, in_specs=[pl.BlockSpec(memory_spac...  6.34 us

profile of v9, /device:TPU:1, one launch (start us, length us, event | category | flops | bytes accessed | tf_op | source)
XLA Modules:
  0.0 98.6 jit_solution(489898241316008684)
XLA Ops:
  0.6 0.0 copy-start
  0.6 0.0 copy-start.3
  0.7 0.0 copy-start.4
  0.7 0.0 copy-start.5
  0.7 2.6 %spread.1 = (f32[320,128]{1,0:T(8,128)S(1)}, f32[2,8,512]{2,1,0:T(8,128)S(1)}, f32[8,512]{1,0:T(8,128)S(1)}, f32[8,24,512]{2,1,0:T(8,128)S(1)}, bf16[8,256,512]{...) custom-call(s32[1,1,8]{2,1,0:T(1,128)} %refs_0_.1, s32[1,1,8]{2,1,0:T(1,128)} %refs_1_.1, f32[2,1,1,8,512]{4,3,2,1,0:T(8,128)} %refs_2_.1, ...), custom_call_target="tpu_custom_call" | custom-call | flops 4000000000 | bytes 24000000 | tf_op jit(solution)/shard_map/spread/pallas_call | solution.py:418
  3.3 0.0 copy-start.2
  3.3 0.0 copy-start.1
  3.3 0.0 copy-start.6
  3.3 23.3 %all_to_all.30 = f32[320,1,128]{2,1,0:T(1,128)S(1)} all-to-all(f32[320,1,128]{2,1,0:T(1,128)S(1)} %bitcast.31), channel_id=1, replica_groups=mesh['gx'=32,'gy'=16] {'gx'}, dimensions={0} | all-to-all | bytes 327680 | tf_op jit(solution)/shard_map/all_to_all | solution.py:433
  26.6 0.0 copy-done
  26.6 0.6 second.1
  27.2 19.3 %all_to_all.31 = f32[352,1,128]{2,1,0:T(1,128)S(1)} all-to-all(f32[352,1,128]{2,1,0:T(1,128)S(1)} %bitcast.26), channel_id=1, replica_groups=mesh['gx'=32,'gy'=16] {'gy'}, dimensions={0} | all-to-all | bytes 360448 | tf_op jit(solution)/shard_map/all_to_all | solution.py:433
  46.5 0.0 copy-done.3
  46.5 0.0 copy-done.4
  46.5 0.0 copy-done.5
  46.5 0.5 third.1
  47.1 12.6 %all_to_all.32 = f32[352,1,128]{2,1,0:T(1,128)S(1)} all-to-all(f32[352,1,128]{2,1,0:T(1,128)S(1)} %bitcast.25), channel_id=1, replica_groups=mesh['gx'=32,'gy'=16] {'gy'}, dimensions={0} | all-to-all | bytes 360448 | tf_op jit(solution)/shard_map/all_to_all | solution.py:433
  59.7 0.0 copy-done.2
  59.7 0.0 copy-start.7
  59.7 0.6 fourth.1
  60.3 13.5 %all_to_all.33 = f32[320,1,128]{2,1,0:T(1,128)S(1)} all-to-all(f32[320,1,128]{2,1,0:T(1,128)S(1)} %bitcast.29), channel_id=1, replica_groups=mesh['gx'=32,'gy'=16] {'gx'}, dimensions={0} | all-to-all | bytes 327680 | tf_op jit(solution)/shard_map/all_to_all | solution.py:433
  73.8 0.0 copy-done.1
  73.8 0.0 copy-done.6
  73.8 1.2 %read.1 = (f32[2,8,512]{2,1,0:T(8,128)S(1)}, f32[16,128]{1,0:T(8,128)S(1)}) custom-call(s32[1,1,8]{2,1,0:T(1,128)S(1)} %get-tuple-element.11.near_tile_ref, f32[320,128]{1,0:T(8,128)S(1)} %bitcast.30, f32[2,1,1,8,512]{4,3,2,1,0:T(8,128)S(1)} %copy-done.6, f32[2,8,512]{2,1,0:T(8,128)S(1)} %get-tuple-element.13.dir_ref, ...), custom_call_target="tpu_custom_call" | custom-call | tf_op jit(solution)/shard_map/read/pallas_call | solution.py:418
  75.0 11.2 %all_to_all.34 = f32[16,1,128]{2,1,0:T(1,128)S(1)} all-to-all(f32[16,1,128]{2,1,0:T(1,128)S(1)} %bitcast.35), channel_id=1, replica_groups=mesh['gx'=32,'gy'=16] {'gy'}, dimensions={0} | all-to-all | bytes 16384 | tf_op jit(solution)/shard_map/all_to_all | solution.py:433
  86.1 11.6 %all_to_all.35 = f32[32,1,128]{2,1,0:T(1,128)S(1)} all-to-all(f32[32,1,128]{2,1,0:T(1,128)S(1)} %bitcast.33), channel_id=1, replica_groups=mesh['gx'=32,'gy'=16] {'gx'}, dimensions={0} | all-to-all | bytes 32768 | tf_op jit(solution)/shard_map/all_to_all | solution.py:433
  97.8 0.0 copy-done.7
  97.8 0.8 update.1
  (1 shorter events, 0.0 us)
Async XLA Ops:
  0.6 26.0 %copy-start = (bf16[256,672]{1,0:T(8,128)(2,1)S(1)}, bf16[256,672]{1,0:T(8,128)(2,1)}, u32[]{:S(2)}) copy-start(bf16[256,672]{1,0:T(8,128)(2,1)} %constant.13.clone.table_ref) | copy-start | bytes 1032196
  0.6 45.9 %copy-start.3 = (bf16[256,624]{1,0:T(8,128)(2,1)S(1)}, bf16[256,624]{1,0:T(8,128)(2,1)}, u32[]{:S(2)}) copy-start(bf16[256,624]{1,0:T(8,128)(2,1)} %constant.14.clone.table_ref) | copy-start | bytes 958468
  0.7 45.9 %copy-start.4 = (bf16[352,384]{1,0:T(8,128)(2,1)S(1)}, bf16[352,384]{1,0:T(8,128)(2,1)}, u32[]{:S(2)}) copy-start(bf16[352,384]{1,0:T(8,128)(2,1)} %constant.15.clone.back_ref) | copy-start | bytes 811012
  0.7 45.9 %copy-start.5 = (f32[8,16,256]{2,1,0:T(8,128)S(1)}, f32[8,16,256]{2,1,0:T(8,128)}, u32[]{:S(2)}) copy-start(f32[8,16,256]{2,1,0:T(8,128)} %spec_ref.1) | copy-start | bytes 393220
  3.3 56.4 %copy-start.2 = (bf16[448,384]{1,0:T(8,128)(2,1)S(1)}, bf16[448,384]{1,0:T(8,128)(2,1)}, u32[]{:S(2)}) copy-start(bf16[448,384]{1,0:T(8,128)(2,1)} %constant.16.clone.table_ref) | copy-start | bytes 1032196
  3.3 70.5 %copy-start.1 = (bf16[256,768]{1,0:T(8,128)(2,1)S(1)}, bf16[256,768]{1,0:T(8,128)(2,1)}, u32[]{:S(2)}) copy-start(bf16[256,768]{1,0:T(8,128)(2,1)} %constant.17.clone.table_ref) | copy-start | bytes 1179652
  3.3 70.5 %copy-start.6 = (f32[2,1,1,8,512]{4,3,2,1,0:T(8,128)S(1)}, f32[2,1,1,8,512]{4,3,2,1,0:T(8,128)}, u32[]{:S(2)}) copy-start(f32[2,1,1,8,512]{4,3,2,1,0:T(8,128)} %res_ref.3) | copy-start | bytes 98308
  59.7 38.0 %copy-start.7 = (f32[2,1,1,8,512]{4,3,2,1,0:T(8,128)S(1)}, f32[2,1,1,8,512]{4,3,2,1,0:T(8,128)}, u32[]{:S(2)}) copy-start(f32[2,1,1,8,512]{4,3,2,1,0:T(8,128)} %iterate_ref.1) | copy-start | bytes 98308
